TPU v7x, 128 devices: a whole 4x4x4 slice. The times are simulated.
128 devices in a mesh: feat: 8 (over z, core), node: 16 (over y, x).
Axes of the slice: x: 4, y: 4, z: 4, core: 2. Of those that a mesh axis runs over, the one named last changes fastest.
Arguments:
- features: bfloat16 [8, 16384, 1024], P(None, 'node', 'feat'), may hold values from -6 to 6
- w_one: bfloat16 [1024, 512], P('feat'), may hold values from -0.1875 to 0.1875
- w_two: bfloat16 [256, 512], replicated, may hold values from -0.375 to 0.375
- b_one: float32 [256], replicated, may hold values from -3 to 3
- b_two: float32 [256], replicated, may hold values from -3 to 3
- owner_one: int32 [8, 8192, 8], P('feat', 'node'), may hold values from 0 to 15, all different within a row; in each aligned block of 512 rows (0 to 511, 512 to 1023, ..., all dimensions but the last counted through in order) at most 384 rows name the same one
- slot_one: int32 [8, 8192, 8], P('feat', 'node'), may hold values from 0 to 1023
- owner_two: int32 [8, 4096, 8], P('feat', 'node'), may hold values from 0 to 15, all different within a row; in each aligned block of 256 rows (0 to 255, 256 to 511, ..., all dimensions but the last counted through in order) at most 192 rows name the same one
- slot_two: int32 [8, 4096, 8], P('feat', 'node'), may hold values from 0 to 511
- cotangent: float32 [8, 4096, 256], P('feat', 'node'), may hold values from -0.3125 to 0.3125
Outputs:
- layer_out: bfloat16 [8, 4096, 256], P('feat', 'node')
- grad_w_one: float32 [1024, 512], P('feat')
- grad_w_two: float32 [256, 512], replicated
- grad_b_one: float32 [256], replicated
Inputs may be any that keep to these rules, and one draw needn't show every extreme that they name: `owner_one`: each row names 8 different owners; within the rows of one device (aligned blocks of 512 rows, in order) no owner is named by more than 384 rows, a bound that some block reaches. `owner_two`: each row names 8 different owners; within the rows of one device (aligned blocks of 256 rows, in order) no owner is named by more than 192 rows, a bound that some block reaches.
All inputs are finite; a program needn't handle non-finite values.
Results may differ from a plain program's by a relative error of at most 0.02.
Values may be sent and summed in bfloat16 or wider, within the bound.
A program may use at most 128 MiB of HBM per device.

v0:
```python
import jax
import jax.numpy as jnp
from jax import lax
from jax.sharding import PartitionSpec as P


def silu_slope(linear):
    logistic = jax.nn.sigmoid(linear)
    return logistic * (1.0 + linear * (1.0 - logistic))


def bucket_places(owners, peers):
    owner_list = owners.reshape(-1)
    onehot = (owner_list[:, None] == jnp.arange(peers, dtype=jnp.int32)[None, :]).astype(jnp.int32)
    before = jnp.cumsum(onehot, axis=0) - onehot
    return (owner_list, jnp.sum(before * onehot, axis=1))


def edge_rows(message, fanout):
    hidden = message.shape[1]
    return jnp.broadcast_to(message[:, None, :], (message.shape[0], fanout, hidden)).reshape(
        -1, hidden
    )


def on_device(
    features, w_one, w_two, b_one, b_two, owner_one, slot_one, owner_two, slot_two, cotangent
):
    peers = lax.axis_size("node")
    rows_one = features.shape[1]
    hidden = w_two.shape[0]
    fanout = owner_one.shape[2]
    rows_two = owner_one.shape[1]
    rows_three = owner_two.shape[1]
    cap_one = min(rows_two, 3 * rows_two * fanout // (2 * peers))
    cap_two = min(rows_three, 3 * rows_three * fanout // (2 * peers))
    list_one, places_one = bucket_places(owner_one[0], peers)
    list_two, places_two = bucket_places(owner_two[0], peers)
    slots_one = slot_one[0].reshape(-1)
    slots_two = slot_two[0].reshape(-1)
    slab_rows = features
    proj_one = lax.psum_scatter(
        jnp.einsum("grf,fh->grh", slab_rows, w_one, preferred_element_type=jnp.float32).astype(
            jnp.bfloat16
        ),
        "feat",
        scatter_dimension=0,
        tiled=True,
    ).astype(jnp.float32)[0]
    table_one = proj_one[:, hidden:].astype(jnp.bfloat16)
    ask_one = jnp.zeros((peers, cap_one), jnp.int32).at[list_one, places_one].set(slots_one)
    ask_two = jnp.zeros((peers, cap_two), jnp.int32).at[list_two, places_two].set(slots_two)
    asked_one, asked_two = (
        lax.all_to_all(ask_one, "node", split_axis=0, concat_axis=0, tiled=True),
        lax.all_to_all(ask_two, "node", split_axis=0, concat_axis=0, tiled=True),
    )
    fetched_one = lax.all_to_all(
        table_one[asked_one], "node", split_axis=0, concat_axis=0, tiled=True
    )
    pulled_one = fetched_one[list_one, places_one]
    mean_one = (
        jnp.sum(pulled_one.reshape(rows_two, fanout, hidden).astype(jnp.float32), axis=1) / fanout
    )
    linear_one = proj_one[:rows_two, :hidden] + b_one + mean_one
    hidden_one = jax.nn.silu(linear_one).astype(jnp.bfloat16)
    proj_two = jnp.dot(hidden_one, w_two, preferred_element_type=jnp.float32)
    table_two = proj_two[:, hidden:].astype(jnp.bfloat16)
    fetched_two = lax.all_to_all(
        table_two[asked_two], "node", split_axis=0, concat_axis=0, tiled=True
    )
    pulled_two = fetched_two[list_two, places_two]
    mean_two = (
        jnp.sum(pulled_two.reshape(rows_three, fanout, hidden).astype(jnp.float32), axis=1) / fanout
    )
    layer_out = (proj_two[:rows_three, :hidden] + b_two + mean_two).astype(jnp.bfloat16)
    grad_out = cotangent[0]
    edge_two = edge_rows((grad_out / fanout).astype(jnp.bfloat16), fanout)
    outgoing_two = (
        jnp.zeros((peers, cap_two, hidden), jnp.bfloat16).at[list_two, places_two].set(edge_two)
    )
    returned_two = lax.all_to_all(outgoing_two, "node", split_axis=0, concat_axis=0, tiled=True)
    grad_table_two = (
        jnp.zeros((rows_two, hidden), jnp.float32)
        .at[asked_two.reshape(-1)]
        .add(returned_two.reshape(-1, hidden).astype(jnp.float32))
    )
    grad_self_two = jnp.concatenate(
        [grad_out, jnp.zeros((rows_two - rows_three, hidden), jnp.float32)], axis=0
    )
    grad_proj_two = jnp.concatenate([grad_self_two, grad_table_two], axis=1).astype(jnp.bfloat16)
    local_w_two = jnp.dot(hidden_one.T, grad_proj_two, preferred_element_type=jnp.float32)
    grad_hidden_one = jnp.dot(grad_proj_two, w_two.T, preferred_element_type=jnp.float32)
    grad_linear_one = grad_hidden_one * silu_slope(linear_one)
    local_b_one = jnp.sum(grad_linear_one, axis=0)
    edge_one = edge_rows((grad_linear_one / fanout).astype(jnp.bfloat16), fanout)
    outgoing_one = (
        jnp.zeros((peers, cap_one, hidden), jnp.bfloat16).at[list_one, places_one].set(edge_one)
    )
    returned_one = lax.all_to_all(outgoing_one, "node", split_axis=0, concat_axis=0, tiled=True)
    grad_table_one = (
        jnp.zeros((rows_one, hidden), jnp.float32)
        .at[asked_one.reshape(-1)]
        .add(returned_one.reshape(-1, hidden).astype(jnp.float32))
    )
    grad_self_one = jnp.concatenate(
        [grad_linear_one, jnp.zeros((rows_one - rows_two, hidden), jnp.float32)], axis=0
    )
    grad_proj_one = jnp.concatenate([grad_self_one, grad_table_one], axis=1).astype(jnp.bfloat16)
    slab_rows = features
    local_w_one = jnp.einsum(
        "grf,grh->fh",
        slab_rows,
        lax.all_gather(grad_proj_one[None], "feat", axis=0, tiled=True),
        preferred_element_type=jnp.float32,
    )
    grad_w_one = lax.psum(local_w_one.astype(jnp.bfloat16), "node").astype(jnp.float32)
    grad_w_two, grad_b_one = lax.psum((local_w_two, local_b_one), ("feat", "node"))
    return (layer_out[None], grad_w_one, grad_w_two, grad_b_one)


def solution(mesh):
    placed = (
        P(None, "node", "feat"),
        P("feat", None),
        P(),
        P(),
        P(),
        P("feat", "node", None),
        P("feat", "node", None),
        P("feat", "node", None),
        P("feat", "node", None),
        P("feat", "node", None),
    )
    return jax.shard_map(
        on_device,
        mesh=mesh,
        in_specs=placed,
        out_specs=(P("feat", "node", None), P("feat", None), P(), P()),
        check_vma=False,
    )
```

profile of v0, /device:TPU:0, one launch (start us, length us, event | category | flops | bytes accessed | tf_op | source)
XLA Modules:
  0.0 640.2 jit_solution(9033650618224502226)
XLA Ops:
  8.8 6.4 %convolution_convert_fusion = bf16[8,1024,512]{2,1,0:T(8,128)(2,1)} fusion(bf16[8,1024,128]{2,1,0:T(8,128)(2,1)S(1)} %copy-done, bf16[128,512]{1,0:T(8,128)(2,1)} %param.11), kind=kOutput, calls=%fused_computation.10 | convolution fusion | flops 1077936128 | bytes 10616832 | tf_op jit(solution)/shard_map/grf,fh->grh/dot_general | solution.py:43
  16.4 4.5 reduce-window.16
  22.3 8.1 %scatter_custom_fusion.3 = s32[3072]{0:T(1024)S(1)} fusion(s32[2048]{0:T(1024)S(1)} %broadcast_select_fusion.1, s32[2048]{0:T(1024)S(1)} %reshape.390, s32[]{:T(128)} %constant.12.clone.1), kind=kCustom, calls=%fused_computation.93 | custom fusion | bytes 12292
  31.0 7.1 %all-to-all-start.2 = ((s32[16,1,192]{2,1,0:T(1,128)}), s32[16,1,192]{2,1,0:T(1,128)S(1)}, u32[]{:S(2)}, u32[]{:S(2)}) async-start(s32[16,1,192]{2,1,0:T(1,128)} %all_to_all.32), calls=%async_computation.3 | async-start | bytes 32768 | tf_op jit(solution)/shard_map/all_to_all | solution.py:55
  38.8 4.6 reduce-window.14
  45.1 16.1 %scatter_custom_fusion.2 = s32[6144]{0:T(1024)} fusion(s32[4096]{0:T(1024)S(1)} %broadcast_select_fusion, s32[4096]{0:T(1024)S(1)} %reshape.384, s32[]{:T(128)} %constant.12.clone.1), kind=kCustom, calls=%fused_computation.88 | custom fusion | bytes 24580
  61.2 7.2 %all-to-all-start = ((s32[16,1,384]{2,1,0:T(1,128)}), s32[16,1,384]{2,1,0:T(1,128)S(1)}, u32[]{:S(2)}, u32[]{:S(2)}) async-start(s32[16,1,384]{2,1,0:T(1,128)} %bitcast.4), calls=%async_computation.1 | async-start | bytes 49152 | tf_op jit(solution)/shard_map/all_to_all | solution.py:54
  68.5 10.6 %scatter_custom_fusion.4 = bf16[3072,256]{1,0:T(8,128)(2,1)} fusion(s32[2048]{0:T(1024)S(1)} %broadcast_select_fusion.1, bf16[]{:T(256)} %constant.21.clone.1, bf16[256,256]{1,0:T(8,128)(2,1)S(1)} %get-tuple-element.19), kind=kCustom, calls=%fused_computation.26 | custom fusion | bytes 1703938
  79.0 7.3 %all-to-all-start.4 = ((bf16[16,192,256]{2,1,0:T(8,128)(2,1)}), bf16[16,192,256]{2,1,0:T(8,128)(2,1)}, u32[]{:S(2)}, u32[]{:S(2)}) async-start(bf16[16,192,256]{2,1,0:T(8,128)(2,1)} %bitcast.104), calls=%async_computation.5 | async-start | bytes 3145728 | tf_op jit(solution)/shard_map/all_to_all | solution.py:81
  87.5 24.9 %gather_fusion = bf16[6144,256]{1,0:T(8,128)(2,1)} fusion(bf16[1024,256]{1,0:T(8,128)(2,1)S(1)} %slice.47, s32[6144]{0:T(1024)S(1)} %broadcast_clamp_fusion), kind=kCustom, calls=%fused_computation | custom fusion | bytes 6316032 | tf_op jit(solution)/shard_map/gather | solution.py:58
  112.4 7.2 %all-to-all-start.1 = ((bf16[16,384,256]{2,1,0:T(8,128)(2,1)}), bf16[16,384,256]{2,1,0:T(8,128)(2,1)}, u32[]{:S(2)}, u32[]{:S(2)}) async-start(bf16[16,384,256]{2,1,0:T(8,128)(2,1)} %bitcast.102), calls=%async_computation.2 | async-start | bytes 6291456 | tf_op jit(solution)/shard_map/all_to_all | solution.py:57
  119.7 16.2 %scatter_custom_fusion = f32[512,256]{1,0:T(8,128)S(1)} fusion(s32[3072]{0:T(1024)S(1)} %bitcast.119, bf16[3072,256]{1,0:T(8,128)(2,1)} %bitcast.34, f32[]{:T(128)} %constant.16.clone.1), kind=kCustom, calls=%fused_computation.14 | custom fusion | flops 1572864 | bytes 2097156 | tf_op jit(solution)/shard_map/scatter-add | solution.py:85
  136.0 26.0 %all-to-all-done.1 = bf16[16,384,256]{2,1,0:T(8,128)(2,1)} async-done(((bf16[16,384,256]{2,1,0:T(8,128)(2,1)}), bf16[16,384,256]{2,1,0:T(8,128)(2,1)}, u32[]{:S(2)}, u32[]{:S(2)}) %all-to-all-start.1) | async-done | bytes 3145760 | tf_op jit(solution)/shard_map/all_to_all | solution.py:57
  162.0 69.0 %gather_fusion.1 = bf16[4096,256]{1,0:T(8,128)(2,1)} fusion(bf16[16,384,256]{2,1,0:T(8,128)(2,1)} %all-to-all-done.1, s32[4096]{0:T(1024)S(1)} %bitcast.100), kind=kCustom, calls=%fused_computation.1 | custom fusion | bytes 4227072 | tf_op jit(solution)/shard_map/gather | solution.py:60
  235.6 20.0 %scatter_custom_fusion.5 = bf16[6144,256]{1,0:T(8,128)(2,1)} fusion(s32[4096]{0:T(1024)S(1)} %broadcast_select_fusion, bf16[]{:T(256)} %constant.21.clone.1, bf16[512,256]{1,0:T(8,128)(2,1)S(1)} %get-tuple-element.17), kind=kCustom, calls=%fused_computation.17 | custom fusion | bytes 3407874
  261.0 42.9 %all-to-all-done.5 = bf16[16,384,256]{2,1,0:T(8,128)(2,1)} async-done(((bf16[16,384,256]{2,1,0:T(8,128)(2,1)}), bf16[16,384,256]{2,1,0:T(8,128)(2,1)}, u32[]{:S(2)}, u32[]{:S(2)}) %all-to-all-start.5) | async-done | bytes 3145760 | tf_op jit(solution)/shard_map/all_to_all | solution.py:99
  303.9 31.3 %scatter_custom_fusion.1 = f32[1024,256]{1,0:T(8,128)S(1)} fusion(s32[6144]{0:T(1024)S(1)} %bitcast.118, bf16[6144,256]{1,0:T(8,128)(2,1)} %bitcast.35, f32[]{:T(128)} %constant.16.clone.1), kind=kCustom, calls=%fused_computation.11 | custom fusion | flops 3145728 | bytes 4194308 | tf_op jit(solution)/shard_map/scatter-add | solution.py:103
  340.0 12.9 %gather_fusion.2 = bf16[3072,256]{1,0:T(8,128)(2,1)} fusion(bf16[512,256]{1,0:T(8,128)(2,1)S(1)} %slice.75, s32[3072]{0:T(1024)S(1)} %broadcast_clamp_fusion.1), kind=kCustom, calls=%fused_computation.2 | custom fusion | bytes 3158016 | tf_op jit(solution)/shard_map/gather | solution.py:69
  353.0 9.5 %all-to-all-start.3 = ((bf16[16,192,256]{2,1,0:T(8,128)(2,1)}), bf16[16,192,256]{2,1,0:T(8,128)(2,1)}, u32[]{:S(2)}, u32[]{:S(2)}) async-start(bf16[16,192,256]{2,1,0:T(8,128)(2,1)} %bitcast.105), calls=%async_computation.4 | async-start | bytes 3145728 | tf_op jit(solution)/shard_map/all_to_all | solution.py:68
  362.5 30.6 %all-gather.2.cloned.1.call-done = bf16[8,1024,512]{2,1,0:T(8,128)(2,1)} async-done(((bf16[1,1024,512]{2,1,0:T(8,128)(2,1)}), bf16[8,1024,512]{2,1,0:T(8,128)(2,1)}) %all-gather.2.cloned.1.call-update) | async-done | bytes 8388624 | tf_op jit(solution)/shard_map/all_gather | solution.py:113
  393.2 6.4 %fusion.8 = bf16[128,512]{0,1:T(8,128)(2,1)} fusion(bf16[8,1024,512]{2,1,0:T(8,128)(2,1)} %all-gather.2.cloned.1.call-done, bf16[8,1024,128]{2,1,0:T(8,128)(2,1)S(1)} %copy-done), kind=kOutput, calls=%fused_computation.23 | convolution fusion | flops 1073807360 | bytes 10616832 | tf_op jit(solution)/shard_map/grf,grh->fh/dot_general | solution.py:110
  401.8 65.4 %psum.23 = f32[256]{0:T(256)} all-reduce(f32[256]{0:T(256)S(1)} %get-tuple-element.16), channel_id=1, replica_groups=mesh['feat'=8,'node'=16] {'feat','node'}, use_global_device_ids=true, to_apply=%region_18.19 | all-reduce | flops 256 | bytes 2048 | tf_op jit(solution)/shard_map/psum | solution.py:117
  467.2 25.2 %gather_fusion.3 = bf16[2048,256]{1,0:T(8,128)(2,1)S(1)} fusion(bf16[16,192,256]{2,1,0:T(8,128)(2,1)} %all-to-all-done.3, s32[2048]{0:T(1024)S(1)} %bitcast.101), kind=kCustom, calls=%fused_computation.3 | custom fusion | bytes 2113536 | tf_op jit(solution)/shard_map/gather | solution.py:71
  496.5 135.3 %all-reduce.7.cloned.1.call-done = f32[256,512]{1,0:T(8,128)} async-done(((f32[256,512]{1,0:T(8,128)}), f32[256,512]{1,0:T(8,128)}) %all-reduce.7.cloned.1.call-update) | async-done | bytes 524304 | tf_op jit(solution)/shard_map/psum | solution.py:117
  (106 shorter events, 31.3 us)
Async XLA Ops:
  7.2 79.2 %reduce-scatter.2.cloned.1.call-start = ((), (), s32[]{:S(2)}) async-start(), calls=%async_computation.7 | async-start | bytes 9437184 | tf_op jit(solution)/shard_map/reduce_scatter | solution.py:42
  15.2 6.4 copy-start.10
  15.2 6.8 %copy-start.15 = (s32[2]{0:T(128)S(1)}, s32[2]{0:T(128)}, u32[]{:S(2)}) copy-start(s32[2]{0:T(128)} %constant.64) | copy-start | bytes 28
  15.2 6.9 %copy-start.14 = (s32[2]{0:T(128)S(1)}, s32[2]{0:T(128)}, u32[]{:S(2)}) copy-start(s32[2]{0:T(128)} %constant.67) | copy-start | bytes 28
  15.2 22.9 %copy-start.7 = (s32[1,512,8]{1,2,0:T(8,128)S(1)}, s32[1,512,8]{1,2,0:T(8,128)}, u32[]{:S(2)}) copy-start(s32[1,512,8]{1,2,0:T(8,128)} %param.15) | copy-start | bytes 49156
  20.9 23.6 %copy-start.13 = (s32[2]{0:T(128)S(1)}, s32[2]{0:T(128)}, u32[]{:S(2)}) copy-start(s32[2]{0:T(128)} %constant.58) | copy-start | bytes 28
  21.0 23.7 %copy-start.12 = (s32[2]{0:T(128)S(1)}, s32[2]{0:T(128)}, u32[]{:S(2)}) copy-start(s32[2]{0:T(128)} %constant.61) | copy-start | bytes 28
  21.4 23.4 %copy-start.8 = (s32[1,512,8]{1,2,0:T(8,128)S(1)}, s32[1,512,8]{1,2,0:T(8,128)}, u32[]{:S(2)}) copy-start(s32[1,512,8]{1,2,0:T(8,128)} %param.16) | copy-start | bytes 49156
  21.9 46.5 %copy-start.4 = (f32[1,256,256]{2,1,0:T(8,128)S(1)}, f32[1,256,256]{2,1,0:T(8,128)}, u32[]{:S(2)}) copy-start(f32[1,256,256]{2,1,0:T(8,128)} %param.19) | copy-start | bytes 786436
  31.0 30.1 %all-to-all-start.2 = ((s32[16,1,192]{2,1,0:T(1,128)}), s32[16,1,192]{2,1,0:T(1,128)S(1)}, u32[]{:S(2)}, u32[]{:S(2)}) async-start(s32[16,1,192]{2,1,0:T(1,128)} %all_to_all.32), calls=%async_computation.3 | async-start | bytes 32768 | tf_op jit(solution)/shard_map/all_to_all | solution.py:55
  61.2 17.8 %all-to-all-start = ((s32[16,1,384]{2,1,0:T(1,128)}), s32[16,1,384]{2,1,0:T(1,128)S(1)}, u32[]{:S(2)}, u32[]{:S(2)}) async-start(s32[16,1,384]{2,1,0:T(1,128)} %bitcast.4), calls=%async_computation.1 | async-start | bytes 49152 | tf_op jit(solution)/shard_map/all_to_all | solution.py:54
  68.5 165.5 %copy-start.5 = (bf16[256,256]{1,0:T(8,128)(2,1)}, bf16[256,256]{1,0:T(8,128)(2,1)S(1)}, u32[]{:S(2)}) copy-start(bf16[256,256]{1,0:T(8,128)(2,1)S(1)} %get-tuple-element.20) | copy-start | bytes 393220
  79.0 33.3 %all-to-all-start.4 = ((bf16[16,192,256]{2,1,0:T(8,128)(2,1)}), bf16[16,192,256]{2,1,0:T(8,128)(2,1)}, u32[]{:S(2)}, u32[]{:S(2)}) async-start(bf16[16,192,256]{2,1,0:T(8,128)(2,1)} %bitcast.104), calls=%async_computation.5 | async-start | bytes 3145728 | tf_op jit(solution)/shard_map/all_to_all | solution.py:81
  112.4 49.6 %all-to-all-start.1 = ((bf16[16,384,256]{2,1,0:T(8,128)(2,1)}), bf16[16,384,256]{2,1,0:T(8,128)(2,1)}, u32[]{:S(2)}, u32[]{:S(2)}) async-start(bf16[16,384,256]{2,1,0:T(8,128)(2,1)} %bitcast.102), calls=%async_computation.2 | async-start | bytes 6291456 | tf_op jit(solution)/shard_map/all_to_all | solution.py:57
  230.9 3.1 copy-start.16
  230.9 3.1 copy-start.17
  255.6 48.3 %all-to-all-start.5 = ((bf16[16,384,256]{2,1,0:T(8,128)(2,1)}), bf16[16,384,256]{2,1,0:T(8,128)(2,1)}, u32[]{:S(2)}, u32[]{:S(2)}) async-start(bf16[16,384,256]{2,1,0:T(8,128)(2,1)} %bitcast.103), calls=%async_computation.6 | async-start | bytes 6291456 | tf_op jit(solution)/shard_map/all_to_all | solution.py:99
  260.0 133.1 %all-gather.2.cloned.1.call-start = ((), (), s32[]{:S(2)}) async-start(), calls=%async_computation.8 | async-start | bytes 9437184 | tf_op jit(solution)/shard_map/all_gather | solution.py:113
  335.2 2.3 copy-start.2
  353.0 114.2 %all-to-all-start.3 = ((bf16[16,192,256]{2,1,0:T(8,128)(2,1)}), bf16[16,192,256]{2,1,0:T(8,128)(2,1)}, u32[]{:S(2)}, u32[]{:S(2)}) async-start(bf16[16,192,256]{2,1,0:T(8,128)(2,1)} %bitcast.105), calls=%async_computation.4 | async-start | bytes 3145728 | tf_op jit(solution)/shard_map/all_to_all | solution.py:68
  362.5 37.2 %copy-start.6 = (bf16[256,256]{1,0:T(8,128)(2,1)S(1)}, bf16[256,256]{1,0:T(8,128)(2,1)}, u32[]{:S(2)}) copy-start(bf16[256,256]{1,0:T(8,128)(2,1)} %copy-done.5) | copy-start | bytes 393220
  362.5 132.3 %all-reduce.5.cloned.1.call-start = ((), (), s32[]{:S(2)}) async-start(), calls=%async_computation.9 | async-start | bytes 262144 | tf_op jit(solution)/shard_map/psum | solution.py:116
  399.6 232.2 %all-reduce.7.cloned.1.call-start = ((), (), s32[]{:S(2)}) async-start(), calls=%async_computation.10 | async-start | bytes 1048576 | tf_op jit(solution)/shard_map/psum | solution.py:117
  467.2 25.9 %copy-start.11 = (f32[256]{0:T(256)S(1)}, f32[256]{0:T(256)}, u32[]{:S(2)}) copy-start(f32[256]{0:T(256)} %param.14) | copy-start | bytes 3076
  (4 other events, 5.0 us)
Sparse Core Ops, SparseCore 0:
  15.4 55.0 reduce-scatter.1
  337.5 55.5 all-gather.1
  399.7 82.0 all-reduce.4
  487.8 144.0 all-reduce.6
where the time goes:
time: 644 us; the launch traced here: 640 us
  waiting for transfers between devices  235 us (36%)
  local copies, waits for them, and re-layouts  199 us (31%)
  other arithmetic  65.9 us (10%)
  blocking collectives  65.4 us (10%)
  starting transfers between devices  42.9 us (7%)
  matrix products  18 us (3%)
  between operations  14.3 us (2%)
    psum x1, waiting for transfers between devices, on_device(): lax.psum((local_w_two, local_b_one), ('feat', 'node'))  135 us
    gather x1, local copies, waits for them, and re-layouts, on_device(): pulled_one = fetched_one[list_one, places_one]  69 us
    psum x1, blocking collectives, on_device(): lax.psum((local_w_two, local_b_one), ('feat', 'node'))  65.4 us
    unnamed x46, local copies, waits for them, and re-layouts  62.1 us
    all_to_all x1, waiting for transfers between devices, on_device(): lax.all_to_all(outgoing_one, 'node', split_axis=0, concat_axis=0, tiled=T...  42.9 us
    scatter-add x1, other arithmetic, on_device(): grad_table_one = jnp.zeros((rows_one, hidden), jnp.float32).at[asked_one....  31.3 us
    all_gather x1, waiting for transfers between devices, on_device(): lax.all_gather(grad_proj_one[None], 'feat', axis=0, tiled=True)  30.6 us
    all_to_all x1, waiting for transfers between devices, on_device(): lax.all_to_all(table_one[asked_one], 'node', split_axis=0, concat_axis=0,...  26 us
  transfers between devices with their start and end apart: 10, of which 4 were waited for; matrix products, arithmetic and copies ran while one was open for 22% of the time, Pallas kernels for 0%

commit v1 on v0

v1 whole, which is shorter than its diff:
```python
import functools

import jax
import jax.numpy as jnp
from jax import lax
from jax.experimental import pallas as pl
from jax.experimental.pallas import tpu as pltpu
from jax.sharding import PartitionSpec as P

MESH = pl.DeviceIdType.MESH
CHUNKS = 4
FEATS = 8
SIDE = 4
BF = jnp.bfloat16
F32 = jnp.float32


def line_place(core, node):
    low, high = node % SIDE, node // SIDE
    return (1 - core) * low + core * high, (1 - core) * high + core * low


def node_at(core, u, v):
    return (1 - core) * (v * SIDE + u) + core * (u * SIDE + v)


def dot(a, b, dims=((1,), (0,))):
    return lax.dot_general(a, b, (dims, ((), ())), preferred_element_type=F32)


def step_kernel(
    feat_ref, w_one_ref, w_two_ref, b_one_ref, b_two_ref, asks_ref, cot_ref,
    out_ref, gw_one_ref, gw_two_ref, gb_ref,
    slab, w_parts, w_full, asks, asks_col, msg_two, gsum_two, gsend_two, grecv_two,
    gproj_two, ghid, table, self_one, ysum, ysend, yrecv, hidden, self_two,
    table_two, ysum_two, ysend_two, yrecv_two, glin, msg_one, gsum, gsend, grecv,
    w_out, w_in, w_mid, v_in, z_out, z_in, piece_all,
    ssem, rsem, lsem,
):
    f, n = lax.axis_index("feat"), lax.axis_index("node")
    core = f % 2
    u, v = line_place(core, n)
    rows_one = slab.shape[1]
    rows_two = asks_col.shape[1] * 2 // 3
    rows_three = rows_two // 2
    fan = 8.0
    part = rows_one // CHUNKS

    def feat_dev(i):
        return ((f + i + FEATS) % FEATS, n)

    def u_dev(d):
        return (f, node_at(core, (u + d + SIDE) % SIDE, v))

    def v_dev(e):
        return (f, node_at(core, u, (v + e + SIDE) % SIDE))

    used = [0]

    def send(src, dst, dev):
        k = used[0]
        used[0] += 1
        copy = pltpu.make_async_remote_copy(
            src_ref=src, dst_ref=dst, send_sem=ssem.at[k], recv_sem=rsem.at[k],
            device_id=dev, device_id_type=MESH,
        )
        copy.start()
        return copy

    started = []

    def keep(copy):
        started.append(copy)
        return copy

    barrier = pltpu.get_barrier_semaphore()
    partners = [feat_dev(i) for i in range(1, FEATS)]
    partners += [u_dev(d) for d in range(1, SIDE)] + [v_dev(e) for e in range(1, SIDE)]
    for dev in partners:
        pl.semaphore_signal(barrier, inc=1, device_id=dev, device_id_type=MESH)
    pl.semaphore_wait(barrier, len(partners))

    ask_copies = {
        e: keep(send(asks_ref.at[e], asks.at[e], v_dev(e))) for e in range(1, SIDE)
    }
    low, high = n % SIDE, n // SIDE
    w_copies = []
    for i in range(1, FEATS):
        their_core = (core + i) % 2
        their_u, their_v = line_place(their_core, n)
        w_copies.append(keep(send(
            w_one_ref.at[pl.ds(pl.multiple_of(high * 32, 32), 32),
                         pl.ds(pl.multiple_of(low * 128, 128), 128)],
            w_parts.at[i, their_u, their_v], feat_dev(i),
        )))
    msg_two[0] = (cot_ref[...] / fan).astype(BF)
    msg_two_copies = {
        e: keep(send(msg_two.at[0], msg_two.at[e], v_dev(e))) for e in range(1, SIDE)
    }
    own = pltpu.make_async_copy(feat_ref.at[f], slab.at[0], lsem)
    own.start()
    slab_copies = []
    for q in range(CHUNKS):
        rows = pl.ds(q * part, part)
        slab_copies.append([
            keep(send(feat_ref.at[(f + i) % FEATS, rows], slab.at[i, rows], feat_dev(i)))
            for i in (4, 5, 3, 2, 6, 7, 1)
        ])

    for copy in w_copies:
        copy.wait_recv()
    along_u = [
        keep(send(w_parts.at[pl.ds(1, FEATS - 1), u, v], w_parts.at[pl.ds(1, FEATS - 1), u, v],
                  u_dev(d)))
        for d in range(1, SIDE)
    ]

    asks[0] = asks_ref[0]
    for e in range(SIDE):
        if e > 0:
            ask_copies[e].wait_recv()
        asks_col[e] = jnp.transpose(asks[e].astype(F32)).astype(jnp.int32)

    def take_two(e, d):
        ids = lax.broadcasted_iota(jnp.int32, (rows_two, rows_three), 0)
        return (ids == asks[e, d:d + 1, rows_two:]).astype(BF)

    for e in range(1, SIDE):
        msg_two_copies[e].wait_recv()
    back_two = {}
    for d in (2, 1, 3, 0):
        total = jnp.zeros((rows_two, 256), F32)
        for e in range(SIDE):
            total += dot(take_two(e, d), msg_two[e])
        if d:
            gsend_two[d - 1] = total.astype(BF)
            back_two[d] = keep(send(gsend_two.at[d - 1], grecv_two.at[d - 1], u_dev(-d)))
        else:
            gsum_two[...] = total

    for copy in along_u:
        copy.wait_recv()
    along_v = [
        keep(send(w_parts.at[pl.ds(1, FEATS - 1), :, v], w_parts.at[pl.ds(1, FEATS - 1), :, v],
                  v_dev(e)))
        for e in range(1, SIDE)
    ]

    for d in range(1, SIDE):
        back_two[d].wait_recv()
    gtab_two = gsum_two[...]
    for d in range(1, SIDE):
        gtab_two += grecv_two[d - 1].astype(F32)
    gproj_two[:rows_three, :256] = cot_ref[...].astype(BF)
    gproj_two[rows_three:, :256] = jnp.zeros((rows_two - rows_three, 256), BF)
    gproj_two[:, 256:] = gtab_two.astype(BF)
    ghid[...] = dot(gproj_two[...], w_two_ref[...], ((1,), (1,)))

    for copy in along_v:
        copy.wait_recv()
    w_full[:128] = w_one_ref[...]
    for i in range(1, FEATS):
        for r in range(4):
            for q in range(4):
                a, b = (1 - core) * q + core * r, (1 - core) * r + core * q
                w_full[i * 128 + r * 32:i * 128 + r * 32 + 32, q * 128:q * 128 + 128] = (
                    w_parts[i, a, b]
                )

    own.wait()
    table_copies = {d: [] for d in range(1, SIDE)}
    for q in range(CHUNKS):
        for copy in slab_copies[q]:
            copy.wait_recv()
        lower = q * part
        block = jnp.concatenate([slab[i, lower:lower + part] for i in range(FEATS)], axis=1)
        if lower < rows_two:
            self_one[lower:lower + part] = dot(block, w_full[:, :256])
        table[0, lower:lower + part] = dot(block, w_full[:, 256:]).astype(BF)
        rows = pl.ds(lower, part)
        for d in (2, 1, 3):
            table_copies[d].append(
                keep(send(table.at[0, rows], table.at[d, rows], u_dev(d)))
            )

    def pick_one(e, d):
        ids = lax.broadcasted_iota(jnp.int32, (rows_two, rows_one), 1)
        return (ids == asks_col[e, :rows_two, d:d + 1]).astype(BF)

    for d in (0, 1, 3):
        if d:
            for copy in table_copies[d]:
                copy.wait_recv()

        def add_line(e, carry, d=d):
            value = dot(pick_one(e, d), table[d])
            ysum[e] = value if d == 0 else ysum[e] + value
            return carry

        lax.fori_loop(0, SIDE, add_line, 0)
    for copy in table_copies[2]:
        copy.wait_recv()
    y_copies = {}
    for e in (2, 1, 3, 0):
        value = ysum[e] + dot(pick_one(e, 2), table[2])
        if e:
            ysend[e - 1] = value.astype(BF)
            y_copies[e] = keep(send(ysend.at[e - 1], yrecv.at[e - 1], v_dev(-e)))
        else:
            ysum[0] = value
    for e in range(1, SIDE):
        y_copies[e].wait_recv()
    total = ysum[0]
    for e in range(1, SIDE):
        total += yrecv[e - 1].astype(F32)
    linear = self_one[...] + b_one_ref[...] + total / fan
    logistic = 1.0 / (1.0 + jnp.exp(-linear))
    hidden[...] = (linear * logistic).astype(BF)
    grad = ghid[...] * (logistic * (1.0 + linear * (1.0 - logistic)))
    glin[...] = grad.astype(BF)
    msg_one[0] = (grad / fan).astype(BF)
    msg_copies = {
        e: keep(send(msg_one.at[0], msg_one.at[e], v_dev(e))) for e in (2, 1, 3)
    }
    bias = jnp.sum(grad, axis=0, keepdims=True)

    proj = dot(hidden[...], w_two_ref[...])
    self_two[...] = proj[:rows_three, :256]
    table_two[0] = proj[:, 256:].astype(BF)
    table_two_copies = {
        d: keep(send(table_two.at[0], table_two.at[d], u_dev(d))) for d in (2, 1, 3)
    }
    gw_two = dot(hidden[...], gproj_two[...], ((0,), (0,))).astype(BF)
    for r in range(4):
        for q in range(4):
            a, b = (1 - core) * q + core * r, (1 - core) * r + core * q
            w_out[a, b, 256:320] = gw_two[r * 64:r * 64 + 64, q * 128:q * 128 + 128]
            if r == 0 and q < 2:
                w_out[a, b, 320:336] = jnp.broadcast_to(
                    bias[:, q * 128:q * 128 + 128], (16, 128)
                ).astype(BF)
            else:
                w_out[a, b, 320:336] = jnp.zeros((16, 128), BF)

    def take_one(e, d):
        ids = lax.broadcasted_iota(jnp.int32, (rows_one, rows_two), 0)
        return (ids == asks[e, pl.ds(d, 1), :rows_two]).astype(BF)

    for e in (0, 1, 3):
        if e:
            msg_copies[e].wait_recv()

        def add_back(d, carry, e=e):
            value = dot(take_one(e, d), msg_one[e])
            gsum[d] = value if e == 0 else gsum[d] + value
            return carry

        lax.fori_loop(0, SIDE, add_back, 0)
    msg_copies[2].wait_recv()
    back_one = {}
    for d in (2, 1, 3, 0):
        value = gsum[d] + dot(take_one(2, d), msg_one[2])
        if d:
            gsend[d - 1] = value.astype(BF)
            back_one[d] = keep(send(gsend.at[d - 1], grecv.at[d - 1], u_dev(-d)))
        else:
            gsum[0] = value

    def pick_two(e, d):
        ids = lax.broadcasted_iota(jnp.int32, (rows_three, rows_two), 1)
        return (ids == asks_col[e, rows_two:, d:d + 1]).astype(BF)

    for d in range(1, SIDE):
        table_two_copies[d].wait_recv()
    y_two = {}
    for e in (2, 1, 3, 0):
        value = jnp.zeros((rows_three, 256), F32)
        for d in range(SIDE):
            value += dot(pick_two(e, d), table_two[d])
        if e:
            ysend_two[e - 1] = value.astype(BF)
            y_two[e] = keep(send(ysend_two.at[e - 1], yrecv_two.at[e - 1], v_dev(-e)))
        else:
            ysum_two[...] = value

    for d in range(1, SIDE):
        back_one[d].wait_recv()
    total = gsum[0]
    for d in range(1, SIDE):
        total += grecv[d - 1].astype(F32)
    gtab = total.astype(BF)
    for half in range(2):
        block = jnp.concatenate([slab[half * 4 + i] for i in range(4)], axis=1)
        left = dot(block[:rows_two], glin[...], ((0,), (0,))).astype(BF)
        right = dot(block, gtab, ((0,), (0,))).astype(BF)
        for i in range(4):
            for r in range(4):
                for q in range(4):
                    a, b = (1 - core) * q + core * r, (1 - core) * r + core * q
                    side = left if q < 2 else right
                    w_out[a, b, (half * 4 + i) * 32:(half * 4 + i) * 32 + 32] = side[
                        i * 128 + r * 32:i * 128 + r * 32 + 32,
                        (q % 2) * 128:(q % 2) * 128 + 128]

    sums = [
        keep(send(w_out.at[(u + d) % SIDE], w_in.at[d - 1], u_dev(d))) for d in (2, 1, 3)
    ]
    for e in range(1, SIDE):
        y_two[e].wait_recv()
    total = ysum_two[...]
    for e in range(1, SIDE):
        total += yrecv_two[e - 1].astype(F32)
    out_ref[...] = (self_two[...] + b_two_ref[...] + total / fan).astype(BF)
    for copy in sums:
        copy.wait_recv()
    total = w_out[u].astype(F32)
    for d in range(1, SIDE):
        total += w_in[d - 1].astype(F32)
    w_mid[...] = total.astype(BF)
    sums = [
        keep(send(w_mid.at[(v + e) % SIDE], v_in.at[e - 1], v_dev(e))) for e in (2, 1, 3)
    ]
    for copy in sums:
        copy.wait_recv()
    total = w_mid[v].astype(F32)
    for e in range(1, SIDE):
        total += v_in[e - 1].astype(F32)
    total = total.astype(BF)
    for i in range(FEATS):
        z_out[i, :32] = total[i * 32:i * 32 + 32]
        z_out[i, 32:] = total[256:]
    sums = [keep(send(z_out.at[i], z_in.at[i - 1], feat_dev(-i))) for i in range(1, FEATS)]
    for copy in sums:
        copy.wait_recv()
    total = z_out[0].astype(F32)
    for i in range(1, FEATS):
        total += z_in[i - 1].astype(F32)
    piece_all[u, v] = total.astype(BF)
    sums = [
        keep(send(piece_all.at[u, v], piece_all.at[u, v], v_dev(e))) for e in range(1, SIDE)
    ]
    for copy in sums:
        copy.wait_recv()
    sums = [keep(send(piece_all.at[u], piece_all.at[u], u_dev(d))) for d in range(1, SIDE)]
    for copy in sums:
        copy.wait_recv()
    for r in range(4):
        for q in range(4):
            a, b = (1 - core) * q + core * r, (1 - core) * r + core * q
            piece = piece_all[a, b].astype(F32)
            gw_one_ref[r * 32:r * 32 + 32, q * 128:q * 128 + 128] = piece[:32]
            gw_two_ref[r * 64:r * 64 + 64, q * 128:q * 128 + 128] = piece[32:96]
            if r == 0 and q < 2:
                gb_ref[:, q * 128:q * 128 + 128] = piece[96:97]
    for copy in started:
        copy.wait_send()


N_COPIES = 3 + 7 + 3 + 7 * CHUNKS + 3 + 3 + 3 + 3 * CHUNKS + 3 * 6 + 3 + 7 + 3 + 3 + 3


def line_asks(owner, slot, core, u, v):
    ids = jnp.stack([
        jnp.stack([node_at(core, (u - d + SIDE) % SIDE, (v + e) % SIDE) for d in range(SIDE)]
                  + [jnp.int32(-1)] * 4)
        for e in range(SIDE)
    ])
    owner_t, slot_t = owner.T, slot.T
    same = owner_t[:, None, None, :] == ids[None, :, :, None]
    return jnp.max(jnp.where(same, slot_t[:, None, None, :], -1), axis=0)


def on_device(
    features, w_one, w_two, b_one, b_two, owner_one, slot_one, owner_two, slot_two, cotangent
):
    f, n = lax.axis_index("feat"), lax.axis_index("node")
    core = f % 2
    u, v = line_place(core, n)
    asks = jnp.concatenate([
        line_asks(owner_one[0], slot_one[0], core, u, v),
        line_asks(owner_two[0], slot_two[0], core, u, v),
    ], axis=2)
    r1, r2, r3 = features.shape[1], owner_one.shape[1], owner_two.shape[1]
    vm = pl.BlockSpec(memory_space=pltpu.VMEM)
    scratch = [
        ((FEATS, r1, 128), BF), ((FEATS, 4, 4, 32, 128), BF), ((1024, 512), BF),
        ((SIDE, 8, r2 + r3), jnp.int32), ((SIDE, r2 + r3, 8), jnp.int32),
        ((SIDE, r3, 256), BF), ((r2, 256), F32), ((3, r2, 256), BF), ((3, r2, 256), BF),
        ((r2, 512), BF), ((r2, 256), F32), ((SIDE, r1, 256), BF), ((r2, 256), F32),
        ((SIDE, r2, 256), F32), ((3, r2, 256), BF), ((3, r2, 256), BF), ((r2, 256), BF),
        ((r3, 256), F32), ((SIDE, r2, 256), BF), ((r3, 256), F32), ((3, r3, 256), BF),
        ((3, r3, 256), BF), ((r2, 256), BF), ((SIDE, r2, 256), BF), ((SIDE, r1, 256), F32),
        ((3, r1, 256), BF), ((3, r1, 256), BF), ((4, 4, 336, 128), BF), ((3, 4, 336, 128), BF),
        ((4, 336, 128), BF), ((3, 336, 128), BF), ((FEATS, 112, 128), BF),
        ((FEATS - 1, 112, 128), BF), ((4, 4, 112, 128), BF),
    ]
    layer_out, gw_one, gw_two, gb = pl.pallas_call(
        step_kernel,
        out_shape=[
            jax.ShapeDtypeStruct((r3, 256), BF), jax.ShapeDtypeStruct((128, 512), F32),
            jax.ShapeDtypeStruct((256, 512), F32), jax.ShapeDtypeStruct((1, 256), F32),
        ],
        in_specs=[pl.BlockSpec(memory_space=pl.ANY)] + [vm] * 6,
        out_specs=[vm] * 4,
        scratch_shapes=[pltpu.VMEM(s, t) for s, t in scratch] + [
            pltpu.SemaphoreType.DMA((N_COPIES,)), pltpu.SemaphoreType.DMA((N_COPIES,)),
            pltpu.SemaphoreType.DMA,
        ],
        compiler_params=pltpu.CompilerParams(
            collective_id=0, has_side_effects=True, vmem_limit_bytes=52 * 2**20
        ),
        cost_estimate=pl.CostEstimate(
            flops=14 * 10**9, bytes_accessed=8 * 2**20, transcendentals=512 * 256
        ),
        name="sage_step",
    )(features, w_one, w_two, b_one[None], b_two[None], asks, cotangent[0])
    return layer_out[None], gw_one, gw_two, gb[0]


def solution(mesh):
    placed = (
        P(None, "node", "feat"),
        P("feat", None),
        P(),
        P(),
        P(),
        P("feat", "node", None),
        P("feat", "node", None),
        P("feat", "node", None),
        P("feat", "node", None),
        P("feat", "node", None),
    )
    return jax.shard_map(
        on_device,
        mesh=mesh,
        in_specs=placed,
        out_specs=(P("feat", "node", None), P("feat", None), P(), P()),
        check_vma=False,
    )
```

time: 644 us -> 134 us (0.21)
  waiting for transfers between devices: 235 us -> 0 us
  local copies, waits for them, and re-layouts: 199 us -> 7.21 us
  Pallas kernels: 0 us -> 124 us
  blocking collectives: 65.4 us -> 0 us
  other arithmetic: 65.9 us -> 1.72 us
  starting transfers between devices: 42.9 us -> 0 us
  matrix products: 18 us -> 0 us
  between operations: 14.3 us -> 0.91 us
    psum x2 -> x0, waiting for transfers between devices: 135 us -> none  [the longest x1 135 us: on_device(): lax.psum((local_w_two, local_b_one), ('feat', 'node'))]
    gather x4 -> x0, local copies, waits for them, and re-layouts: 132 us -> none  [the longest x1 69 us: on_device(): pulled_one = fetched_one[list_one, places_one]]
    pallas_call x0 -> x1, Pallas kernels: none -> 124 us  [on_device(): pl.pallas_call(step_kernel, out_shape=[jax.ShapeDtypeStruct((r3, 256), BF...]
    all_to_all x6 -> x0, waiting for transfers between devices: 68.9 us -> none  [the longest x1 42.9 us: on_device(): lax.all_to_all(outgoing_one, 'node', split_axis=0, concat_axis=0, tiled=T...]
    psum x1 -> x0, blocking collectives: 65.4 us -> none  [on_device(): lax.psum((local_w_two, local_b_one), ('feat', 'node'))]
    unnamed x46 -> x14, local copies, waits for them, and re-layouts: 62.1 us -> 6.87 us
    scatter-add x2 -> x0, other arithmetic: 47.5 us -> none  [the longest x1 31.3 us: on_device(): grad_table_one = jnp.zeros((rows_one, hidden), jnp.float32).at[asked_one....]
    all_to_all x6 -> x0, starting transfers between devices: 42.8 us -> none  [the longest x1 9.48 us: on_device(): lax.all_to_all(table_two[asked_two], 'node', split_axis=0, concat_axis=0,...]
  transfers between devices with their start and end apart: 10 -> 0, of which waited for: 4 -> 0; matrix products, arithmetic and copies ran while one was open for 22% -> 0% of each run, Pallas kernels for 0% -> 0%
where the time goes in v1:
time: 134 us
  Pallas kernels  124 us (93%)
  local copies, waits for them, and re-layouts  7.21 us (5%)
  other arithmetic  1.72 us (1%)
    pallas_call x1, Pallas kernels, on_device(): pl.pallas_call(step_kernel, out_shape=[jax.ShapeDtypeStruct((r3, 256), BF...  124 us
    unnamed x14, local copies, waits for them, and re-layouts  6.87 us

profile of v1, /device:TPU:0, one launch (start us, length us, event | category | flops | bytes accessed | tf_op | source)
XLA Modules:
  0.0 133.7 jit_solution(3679083842107651825)
XLA Ops:
  0.9 0.1 stack.122
  1.0 0.1 stack.116
  1.0 0.1 stack.110
  1.1 0.1 stack.104
  1.2 0.8 select_reduce_fusion.1
  2.1 0.9 select_reduce_fusion
  3.0 0.0 copy-start
  3.0 0.9 copy-done
  3.9 0.0 copy-start.1
  3.9 0.9 copy-done.1
  4.9 0.0 copy-start.2
  4.9 0.9 copy-done.2
  5.8 0.0 copy-start.3
  5.8 0.7 copy-done.3
  6.4 0.0 copy-start.4
  6.4 0.7 copy-done.4
  7.1 123.8 %sage_step.1 = (bf16[256,256]{1,0:T(8,128)(2,1)S(1)}, f32[128,512]{1,0:T(8,128)S(1)}, f32[256,512]{1,0:T(8,128)S(1)}, f32[1,256]{1,0:T(1,128)S(1)}) custom-call(bf16[8,1024,128]{2,1,0:T(8,128)(2,1)} %feat_ref.1, bf16[128,512]{1,0:T(8,128)(2,1)S(1)} %copy-done.2, bf16[256,512]{1,0:T(8,128)(2,1)S(1)} %copy-done, f32[1,256]{1,0:T(1,128)S(1)} %bitcast.40, ...), custom_call_target="tpu_custom_call" | custom-call | flops 14000000000 | bytes 8388608 | tf_op jit(solution)/shard_map/sage_step/pallas_call | solution.py:397
  131.0 0.7 copy.18
  131.6 0.7 copy.19
  132.3 0.8 copy.20
  133.1 0.6 copy.21
  (3 shorter events, 0.0 us)
Async XLA Ops:
  3.0 1.0 copy-start
  3.9 0.9 copy-start.1
  4.9 0.9 copy-start.2
  5.8 0.7 copy-start.3
  6.4 0.7 copy-start.4

commit v2 on v0

v2 whole, which is shorter than its diff:
```python
import jax
import jax.numpy as jnp
from jax import lax
from jax.experimental import pallas as pl
from jax.experimental.pallas import tpu as pltpu
from jax.sharding import PartitionSpec as P

MESH = pl.DeviceIdType.MESH
CHUNKS = 4
HALVES = 2
FEATS = 8
SIDE = 4
FAN = 8
BF = jnp.bfloat16
F32 = jnp.float32
I32 = jnp.int32


def line_place(core, node):
    low, high = node % SIDE, node // SIDE
    return (1 - core) * low + core * high, (1 - core) * high + core * low


def node_at(core, u, v):
    return (1 - core) * (v * SIDE + u) + core * (u * SIDE + v)


def dot(a, b, dims=((1,), (0,))):
    return lax.dot_general(a, b, (dims, ((), ())), preferred_element_type=F32)


def add_up(first, others):
    total = first
    for other in others:
        total += other.astype(F32)
    return total


def step_kernel(
    feat_ref, w_one_ref, w_two_ref, b_one_ref, b_two_ref, owner_one_ref, slot_one_ref,
    owner_two_ref, slot_two_ref, cot_ref,
    out_ref, gw_one_ref, gw_two_ref, gb_ref,
    slab, w_parts, w_full, w_two, b_one, b_two, own_one, slo_one, own_two, slo_two, cot,
    asks_out, asks, asks_col, msg_two, gsum_two, gsend_two, grecv_two,
    gproj_two, ghid, table, self_one, ysum, ysend, yrecv, hidden, self_two,
    table_two, ysum_two, ysend_two, yrecv_two, glin, msg_one, gsum, gsend, grecv,
    two_out, two_in, two_mid, two_u, two_z, two_all,
    pair_out, pair_in, w_out, w_in, w_mid, v_in, z_out, z_in, piece_all,
    ssem, rsem, lsem,
):
    f, n = lax.axis_index("feat"), lax.axis_index("node")
    z, core = f // 2, f % 2
    u, v = line_place(core, n)
    rows_one = slab.shape[1]
    rows_two = own_one.shape[0]
    rows_three = own_two.shape[0]
    part = rows_one // CHUNKS
    half = rows_two // HALVES
    slots = [(dz, dc) for dz in range(4) for dc in range(2)]
    by_far = (2, 1, 3)

    def feat_dev(dz, dc):
        return (((z + dz + 4) % 4) * 2 + (core + dc) % 2, n)

    def u_dev(d):
        return (f, node_at(core, (u + d + SIDE) % SIDE, v))

    def v_dev(e):
        return (f, node_at(core, u, (v + e + SIDE) % SIDE))

    def place(r, q):
        return (1 - core) * q + core * r, (1 - core) * r + core * q

    started = []

    def send(src, dst, dev):
        k = len(started)
        copy = pltpu.make_async_remote_copy(
            src_ref=src, dst_ref=dst, send_sem=ssem.at[k], recv_sem=rsem.at[k],
            device_id=dev, device_id_type=MESH,
        )
        copy.start()
        started.append(copy)
        return copy

    barrier = pltpu.get_barrier_semaphore()
    partners = [feat_dev(*s) for s in slots[1:]]
    partners += [u_dev(d) for d in range(1, SIDE)] + [v_dev(e) for e in range(1, SIDE)]
    for dev in partners:
        pl.semaphore_signal(barrier, inc=1, device_id=dev, device_id_type=MESH)

    loads = []

    def load(src, dst):
        copy = pltpu.make_async_copy(src, dst, lsem.at[len(loads)])
        copy.start()
        loads.append(copy)
        return copy

    index_loads = [
        load(owner_one_ref, own_one), load(slot_one_ref, slo_one),
        load(owner_two_ref, own_two), load(slot_two_ref, slo_two),
    ]
    cot_load = load(cot_ref, cot)
    w_one_load = load(w_one_ref, w_full.at[pl.ds(0, 128)])
    own_load = load(feat_ref.at[f], slab.at[0])
    small_loads = [load(w_two_ref, w_two), load(b_one_ref, b_one), load(b_two_ref, b_two)]

    for copy in index_loads:
        copy.wait()
    for own, slo, lower in ((own_one, slo_one, 0), (own_two, slo_two, rows_two)):
        owner_t = jnp.transpose(own[...].astype(F32))
        slot_t = jnp.transpose(slo[...].astype(F32))
        for e in range(SIDE):
            for d in range(SIDE):
                at = node_at(core, (u - d + SIDE) % SIDE, (v + e) % SIDE)
                found = jnp.max(
                    jnp.where(owner_t == at.astype(F32), slot_t, -1.0), axis=0, keepdims=True
                )
                asks_out[e, d:d + 1, lower:lower + own.shape[0]] = found.astype(I32)
    for e in range(SIDE):
        asks_out[e, SIDE:] = jnp.full((8 - SIDE, rows_two + rows_three), -1, I32)
    cot_load.wait()
    msg_two[0] = (cot[...] / FAN).astype(BF)

    pl.semaphore_wait(barrier, len(partners))

    low, high = n % SIDE, n // SIDE
    w_copies = []
    for i, (dz, dc) in enumerate(slots):
        if i:
            their_u, their_v = line_place((core + dc) % 2, n)
            w_copies.append(send(
                w_one_ref.at[pl.ds(pl.multiple_of(high * 32, 32), 32),
                             pl.ds(pl.multiple_of(low * 128, 128), 128)],
                w_parts.at[i, their_u, their_v], feat_dev(dz, dc),
            ))
    ask_copies = [send(asks_out.at[e], asks.at[e], v_dev(e)) for e in range(1, SIDE)]
    msg_two_copies = [send(msg_two.at[0], msg_two.at[e], v_dev(e)) for e in range(1, SIDE)]
    slab_copies = []
    for c in range(CHUNKS):
        rows = pl.ds(c * part, part)
        slab_copies.append([])
        for i in (4, 5, 2, 3, 6, 7, 1):
            dev = feat_dev(*slots[i])
            slab_copies[c].append(send(feat_ref.at[dev[0], rows], slab.at[i, rows], dev))

    for copy in w_copies:
        copy.wait_recv()
    mine = w_parts.at[pl.ds(1, FEATS - 1), u, v]
    along_u = [send(mine, mine, u_dev(d)) for d in range(1, SIDE)]
    asks[0] = asks_out[0]
    for copy in ask_copies:
        copy.wait_recv()
    for e in range(SIDE):
        asks_col[e] = jnp.transpose(asks[e].astype(F32)).astype(I32)
    for copy in along_u:
        copy.wait_recv()
    mine = w_parts.at[pl.ds(1, FEATS - 1), :, v]
    along_v = [send(mine, mine, v_dev(e)) for e in range(1, SIDE)]

    for copy in msg_two_copies:
        copy.wait_recv()
    msgs = jnp.concatenate([msg_two[e] for e in range(SIDE)], axis=0)
    back_two = []
    for d in (2, 1, 3, 0):
        ids = lax.broadcasted_iota(I32, (rows_two, rows_three), 0)
        picks = jnp.concatenate(
            [(ids == asks[e, d:d + 1, rows_two:]).astype(BF) for e in range(SIDE)], axis=1
        )
        total = dot(picks, msgs)
        if d:
            gsend_two[d - 1] = total.astype(BF)
            back_two.append(send(gsend_two.at[d - 1], grecv_two.at[d - 1], u_dev(-d)))
        else:
            gsum_two[...] = total

    for copy in along_v:
        copy.wait_recv()
    w_one_load.wait()
    for i in range(1, FEATS):
        for r in range(4):
            for q in range(4):
                a, b = place(r, q)
                w_full[i * 128 + r * 32:i * 128 + r * 32 + 32, q * 128:q * 128 + 128] = (
                    w_parts[i, a, b]
                )

    table_copies = []

    def project(c):
        for copy in slab_copies[c]:
            copy.wait_recv()
        lower = c * part
        block = jnp.concatenate([slab[i, lower:lower + part] for i in range(FEATS)], axis=1)
        table[0, lower:lower + part] = dot(block, w_full[:, 256:]).astype(BF)
        rows = pl.ds(lower, part)
        table_copies.append(
            [send(table.at[0, rows], table.at[d, rows], u_dev(d)) for d in by_far]
        )
        if lower < rows_two:
            self_one[lower:lower + part] = dot(block, w_full[:, :256])

    def line_sums(c, e, lower, count):
        ids = lax.broadcasted_iota(I32, (count, part), 1) + c * part
        picks = jnp.concatenate(
            [(ids == asks_col[e, lower:lower + count, d:d + 1]).astype(BF)
             for d in range(SIDE)], axis=1
        )
        rows = jnp.concatenate(
            [table[d, c * part:c * part + part] for d in range(SIDE)], axis=0
        )
        return dot(picks, rows)

    def add_lines(c):
        for copy in table_copies[c]:
            copy.wait_recv()

        def one(e, carry):
            value = line_sums(c, e, 0, rows_two)
            ysum[e] = value if c == 0 else ysum[e] + value
            return carry

        lax.fori_loop(0, SIDE, one, 0)

    own_load.wait()
    for c in range(CHUNKS):
        project(c)
        if c:
            add_lines(c - 1)
        if c == 1:
            for copy in back_two:
                copy.wait_recv()
            for copy in small_loads:
                copy.wait()
            gtab_two = add_up(gsum_two[...], [grecv_two[d] for d in range(SIDE - 1)])
            gproj_two[:rows_three, :256] = cot[...].astype(BF)
            gproj_two[rows_three:, :256] = jnp.zeros((rows_two - rows_three, 256), BF)
            gproj_two[:, 256:] = gtab_two.astype(BF)
            ghid[...] = dot(gproj_two[...], w_two[...], ((1,), (1,)))
    last = CHUNKS - 1
    for copy in table_copies[last]:
        copy.wait_recv()
    y_copies = []
    for h in range(HALVES):
        rows = pl.ds(h * half, half)
        y_copies.append([])
        for e in (2, 1, 3, 0):
            value = ysum[e, h * half:h * half + half] + line_sums(last, e, h * half, half)
            if e:
                ysend[e - 1, h * half:h * half + half] = value.astype(BF)
                y_copies[h].append(
                    send(ysend.at[e - 1, rows], yrecv.at[e - 1, rows], v_dev(-e))
                )
            else:
                ysum[0, h * half:h * half + half] = value
    msg_copies = []
    bias = jnp.zeros((1, 256), F32)
    for h in range(HALVES):
        for copy in y_copies[h]:
            copy.wait_recv()
        rows = slice(h * half, h * half + half)
        total = add_up(ysum[0, rows], [yrecv[e, rows] for e in range(SIDE - 1)])
        linear = self_one[rows] + b_one[...] + total / FAN
        logistic = 1.0 / (1.0 + jnp.exp(-linear))
        grad = ghid[rows] * (logistic * (1.0 + linear * (1.0 - logistic)))
        msg_one[0, rows] = (grad / FAN).astype(BF)
        there = pl.ds(h * half, half)
        msg_copies.append([
            send(msg_one.at[0, there], msg_one.at[e, there], v_dev(e)) for e in by_far
        ])
        glin[rows] = grad.astype(BF)
        hidden[rows] = (linear * logistic).astype(BF)
        bias += jnp.sum(grad, axis=0, keepdims=True)

    proj = dot(hidden[...], w_two[...])
    table_two[0] = proj[:, 256:].astype(BF)
    table_two_copies = [send(table_two.at[0], table_two.at[d], u_dev(d)) for d in by_far]
    self_two[...] = proj[:rows_three, :256]
    gw_two = dot(hidden[...], gproj_two[...], ((0,), (0,))).astype(BF)
    for r in range(4):
        for q in range(4):
            a, b = place(r, q)
            two_out[a, b, :64] = gw_two[r * 64:r * 64 + 64, q * 128:q * 128 + 128]
            if r == 0 and q < 2:
                two_out[a, b, 64:] = jnp.broadcast_to(
                    bias[:, q * 128:q * 128 + 128], (16, 128)
                ).astype(BF)
            else:
                two_out[a, b, 64:] = jnp.zeros((16, 128), BF)
    two_copies = [
        send(two_out.at[:, (v + e) % SIDE], two_in.at[e - 1], v_dev(e)) for e in by_far
    ]

    def line_grads(h, d):
        ids = lax.broadcasted_iota(I32, (rows_one, half), 0)
        picks = jnp.concatenate(
            [(ids == asks[e, pl.ds(d, 1), h * half:h * half + half]).astype(BF)
             for e in range(SIDE)], axis=1
        )
        rows = jnp.concatenate(
            [msg_one[e, h * half:h * half + half] for e in range(SIDE)], axis=0
        )
        return dot(picks, rows)

    for h in range(HALVES - 1):
        for copy in msg_copies[h]:
            copy.wait_recv()

        def add_back(d, carry, h=h):
            value = line_grads(h, d)
            gsum[d] = value if h == 0 else gsum[d] + value
            return carry

        lax.fori_loop(0, SIDE, add_back, 0)
    for copy in msg_copies[HALVES - 1]:
        copy.wait_recv()
    back_one = []
    for d in (2, 1, 3, 0):
        value = gsum[d] + line_grads(HALVES - 1, d)
        if d:
            gsend[d - 1] = value.astype(BF)
            back_one.append(send(gsend.at[d - 1], grecv.at[d - 1], u_dev(-d)))
        else:
            gsum[0] = value

    for copy in two_copies:
        copy.wait_recv()
    for a in range(SIDE):
        two_mid[a] = add_up(
            two_out[a, v].astype(F32), [two_in[e, a] for e in range(SIDE - 1)]
        ).astype(BF)
    two_copies = [
        send(two_mid.at[(u + d) % SIDE], two_u.at[d - 1], u_dev(d)) for d in by_far
    ]

    for copy in table_two_copies:
        copy.wait_recv()
    y_two = []
    rows = jnp.concatenate([table_two[d] for d in range(SIDE)], axis=0)
    for e in (2, 1, 3, 0):
        ids = lax.broadcasted_iota(I32, (rows_three, rows_two), 1)
        picks = jnp.concatenate(
            [(ids == asks_col[e, rows_two:, d:d + 1]).astype(BF) for d in range(SIDE)], axis=1
        )
        value = dot(picks, rows)
        if e:
            ysend_two[e - 1] = value.astype(BF)
            y_two.append(send(ysend_two.at[e - 1], yrecv_two.at[e - 1], v_dev(-e)))
        else:
            ysum_two[...] = value

    for copy in two_copies:
        copy.wait_recv()
    two_z[0] = add_up(two_mid[u].astype(F32), [two_u[d] for d in range(SIDE - 1)]).astype(BF)
    two_copies = [send(two_z.at[0], two_z.at[i], feat_dev(*slots[i])) for i in range(1, FEATS)]

    for copy in y_two:
        copy.wait_recv()
    total = add_up(ysum_two[...], [yrecv_two[e] for e in range(SIDE - 1)])
    out_ref[...] = (self_two[...] + b_two[...] + total / FAN).astype(BF)

    for copy in two_copies:
        copy.wait_recv()
    two_all[u, v] = add_up(
        two_z[0].astype(F32), [two_z[i] for i in range(1, FEATS)]
    ).astype(BF)
    two_copies = [send(two_all.at[u, v], two_all.at[u, v], v_dev(e)) for e in by_far]

    for copy in back_one:
        copy.wait_recv()
    gtab = add_up(gsum[0], [grecv[d] for d in range(SIDE - 1)]).astype(BF)

    def outer(dc):
        block = jnp.concatenate([slab[2 * dz + dc] for dz in range(4)], axis=1)
        return (dot(block[:rows_two], glin[...], ((0,), (0,))),
                dot(block, gtab, ((0,), (0,))))

    left, right = outer(1)
    pair_out[:, :256] = left.astype(BF)
    pair_out[:, 256:] = right.astype(BF)
    pair = send(pair_out, pair_in, feat_dev(0, 1))
    left, right = outer(0)
    for copy in two_copies:
        copy.wait_recv()
    two_copies = [send(two_all.at[u], two_all.at[u], u_dev(d)) for d in by_far]
    pair.wait_recv()
    left = (left + pair_in[:, :256].astype(F32)).astype(BF)
    right = (right + pair_in[:, 256:].astype(F32)).astype(BF)
    for dz in range(4):
        for r in range(4):
            for q in range(4):
                a, b = place(r, q)
                side = left if q < 2 else right
                w_out[a, b, dz * 32:dz * 32 + 32] = side[
                    dz * 128 + r * 32:dz * 128 + r * 32 + 32,
                    (q % 2) * 128:(q % 2) * 128 + 128]

    sums = [send(w_out.at[(u + d) % SIDE], w_in.at[d - 1], u_dev(d)) for d in by_far]
    for copy in two_copies:
        copy.wait_recv()
    for r in range(4):
        for q in range(4):
            a, b = place(r, q)
            piece = two_all[a, b].astype(F32)
            gw_two_ref[r * 64:r * 64 + 64, q * 128:q * 128 + 128] = piece[:64]
            if r == 0 and q < 2:
                gb_ref[:, q * 128:q * 128 + 128] = piece[64:65]
    for copy in sums:
        copy.wait_recv()
    for b in range(SIDE):
        w_mid[b] = add_up(
            w_out[u, b].astype(F32), [w_in[d, b] for d in range(SIDE - 1)]
        ).astype(BF)
    sums = [send(w_mid.at[(v + e) % SIDE], v_in.at[e - 1], v_dev(e)) for e in by_far]
    for copy in sums:
        copy.wait_recv()
    z_out[...] = add_up(w_mid[v].astype(F32), [v_in[e] for e in range(SIDE - 1)]).astype(BF)
    sums = [
        send(z_out.at[pl.ds(dz * 32, 32)], z_in.at[dz - 1], feat_dev(-dz, 0)) for dz in by_far
    ]
    for copy in sums:
        copy.wait_recv()
    piece_all[u, v] = add_up(
        z_out[:32].astype(F32), [z_in[dz] for dz in range(3)]
    ).astype(BF)
    sums = [send(piece_all.at[u, v], piece_all.at[u, v], v_dev(e)) for e in by_far]
    for copy in sums:
        copy.wait_recv()
    sums = [send(piece_all.at[u], piece_all.at[u], u_dev(d)) for d in by_far]
    for copy in sums:
        copy.wait_recv()
    for r in range(4):
        for q in range(4):
            a, b = place(r, q)
            gw_one_ref[r * 32:r * 32 + 32, q * 128:q * 128 + 128] = piece_all[a, b].astype(F32)
    for copy in started:
        copy.wait_send()


N_COPIES = 7 * (3 + CHUNKS) + 3 * (CHUNKS + 2 * HALVES) + 3 * 18


def on_device(
    features, w_one, w_two, b_one, b_two, owner_one, slot_one, owner_two, slot_two, cotangent
):
    r1, r2, r3 = features.shape[1], owner_one.shape[1], owner_two.shape[1]
    vm = pl.BlockSpec(memory_space=pltpu.VMEM)
    scratch = [
        ((FEATS, r1, 128), BF), ((FEATS, 4, 4, 32, 128), BF), ((1024, 512), BF),
        ((256, 512), BF), ((1, 256), F32), ((1, 256), F32),
        ((r2, FAN), I32), ((r2, FAN), I32), ((r3, FAN), I32), ((r3, FAN), I32),
        ((r3, 256), F32), ((SIDE, 8, r2 + r3), I32),
        ((SIDE, 8, r2 + r3), I32), ((SIDE, r2 + r3, 8), I32),
        ((SIDE, r3, 256), BF), ((r2, 256), F32), ((3, r2, 256), BF), ((3, r2, 256), BF),
        ((r2, 512), BF), ((r2, 256), F32), ((SIDE, r1, 256), BF), ((r2, 256), F32),
        ((SIDE, r2, 256), F32), ((3, r2, 256), BF), ((3, r2, 256), BF), ((r2, 256), BF),
        ((r3, 256), F32), ((SIDE, r2, 256), BF), ((r3, 256), F32), ((3, r3, 256), BF),
        ((3, r3, 256), BF), ((r2, 256), BF), ((SIDE, r2, 256), BF), ((SIDE, r1, 256), F32),
        ((3, r1, 256), BF), ((3, r1, 256), BF),
        ((4, 4, 80, 128), BF), ((3, 4, 80, 128), BF), ((4, 80, 128), BF), ((3, 80, 128), BF),
        ((FEATS, 80, 128), BF), ((4, 4, 80, 128), BF),
        ((512, 512), BF), ((512, 512), BF), ((4, 4, 128, 128), BF), ((3, 4, 128, 128), BF),
        ((4, 128, 128), BF), ((3, 128, 128), BF), ((128, 128), BF), ((3, 32, 128), BF),
        ((4, 4, 32, 128), BF),
    ]
    layer_out, gw_one, gw_two, gb = pl.pallas_call(
        step_kernel,
        out_shape=[
            jax.ShapeDtypeStruct((r3, 256), BF), jax.ShapeDtypeStruct((128, 512), F32),
            jax.ShapeDtypeStruct((256, 512), F32), jax.ShapeDtypeStruct((1, 256), F32),
        ],
        in_specs=[pl.BlockSpec(memory_space=pl.ANY)] * 10,
        out_specs=[vm] * 4,
        scratch_shapes=[pltpu.VMEM(s, t) for s, t in scratch] + [
            pltpu.SemaphoreType.DMA((N_COPIES,)), pltpu.SemaphoreType.DMA((N_COPIES,)),
            pltpu.SemaphoreType.DMA((10,)),
        ],
        compiler_params=pltpu.CompilerParams(
            collective_id=0, has_side_effects=True, vmem_limit_bytes=56 * 2**20
        ),
        cost_estimate=pl.CostEstimate(
            flops=14 * 10**9, bytes_accessed=8 * 2**20, transcendentals=512 * 256
        ),
        name="sage_step",
    )(features, w_one, w_two, b_one[None], b_two[None], owner_one[0], slot_one[0],
      owner_two[0], slot_two[0], cotangent[0])
    return layer_out[None], gw_one, gw_two, gb[0]


def solution(mesh):
    placed = (
        P(None, "node", "feat"),
        P("feat", None),
        P(),
        P(),
        P(),
        P("feat", "node", None),
        P("feat", "node", None),
        P("feat", "node", None),
        P("feat", "node", None),
        P("feat", "node", None),
    )
    return jax.shard_map(
        on_device,
        mesh=mesh,
        in_specs=placed,
        out_specs=(P("feat", "node", None), P("feat", None), P(), P()),
        check_vma=False,
    )
```

time: 644 us -> 135 us (0.21)
  waiting for transfers between devices: 235 us -> 0 us
  local copies, waits for them, and re-layouts: 199 us -> 12.4 us
  Pallas kernels: 0 us -> 121 us
  other arithmetic: 65.9 us -> 0 us
  blocking collectives: 65.4 us -> 0 us
  starting transfers between devices: 42.9 us -> 0 us
  matrix products: 18 us -> 0 us
  between operations: 14.3 us -> 0.64 us
    psum x2 -> x0, waiting for transfers between devices: 135 us -> none  [the longest x1 135 us: on_device(): lax.psum((local_w_two, local_b_one), ('feat', 'node'))]
    gather x4 -> x0, local copies, waits for them, and re-layouts: 132 us -> none  [the longest x1 69 us: on_device(): pulled_one = fetched_one[list_one, places_one]]
    pallas_call x0 -> x1, Pallas kernels: none -> 121 us  [on_device(): pl.pallas_call(step_kernel, out_shape=[jax.ShapeDtypeStruct((r3, 256), BF...]
    all_to_all x6 -> x0, waiting for transfers between devices: 68.9 us -> none  [the longest x1 42.9 us: on_device(): lax.all_to_all(outgoing_one, 'node', split_axis=0, concat_axis=0, tiled=T...]
    psum x1 -> x0, blocking collectives: 65.4 us -> none  [on_device(): lax.psum((local_w_two, local_b_one), ('feat', 'node'))]
    unnamed x46 -> x8, local copies, waits for them, and re-layouts: 62.1 us -> 12.4 us
    scatter-add x2 -> x0, other arithmetic: 47.5 us -> none  [the longest x1 31.3 us: on_device(): grad_table_one = jnp.zeros((rows_one, hidden), jnp.float32).at[asked_one....]
    all_to_all x6 -> x0, starting transfers between devices: 42.8 us -> none  [the longest x1 9.48 us: on_device(): lax.all_to_all(table_two[asked_two], 'node', split_axis=0, concat_axis=0,...]
  transfers between devices with their start and end apart: 10 -> 0, of which waited for: 4 -> 0; matrix products, arithmetic and copies ran while one was open for 22% -> 0% of each run, Pallas kernels for 0% -> 0%
where the time goes in v2:
time: 135 us; the launch traced here: 134 us
  Pallas kernels  121 us (90%)
  local copies, waits for them, and re-layouts  12.4 us (9%)
    pallas_call x1, Pallas kernels, on_device(): pl.pallas_call(step_kernel, out_shape=[jax.ShapeDtypeStruct((r3, 256), BF...  121 us
    unnamed x8, local copies, waits for them, and re-layouts  12.4 us

profile of v2, /device:TPU:0, one launch (start us, length us, event | category | flops | bytes accessed | tf_op | source)
XLA Modules:
  0.0 133.8 jit_solution(421133228708474758)
XLA Ops:
  0.6 1.5 %copy.16 = s32[1,256,8]{2,1,0:T(8,128)} copy(s32[1,256,8]{1,2,0:T(8,128)} %param.17) | data formatting | bytes 16384 | tf_op args[7]
  2.1 1.5 %copy.17 = s32[1,256,8]{2,1,0:T(8,128)} copy(s32[1,256,8]{1,2,0:T(8,128)} %param.18) | data formatting | bytes 16384 | tf_op args[8]
  3.6 1.6 %copy.14 = s32[1,512,8]{2,1,0:T(8,128)} copy(s32[1,512,8]{1,2,0:T(8,128)} %param.15) | data formatting | bytes 32768 | tf_op args[5]
  5.2 1.6 %copy.15 = s32[1,512,8]{2,1,0:T(8,128)} copy(s32[1,512,8]{1,2,0:T(8,128)} %param.16) | data formatting | bytes 32768 | tf_op args[6]
  6.7 120.7 %sage_step.1 = (bf16[256,256]{1,0:T(8,128)(2,1)}, f32[128,512]{1,0:T(8,128)}, f32[256,512]{1,0:T(8,128)}, f32[1,256]{1,0:T(1,128)}) custom-call(bf16[8,1024,128]{2,1,0:T(8,128)(2,1)} %feat_ref.1, bf16[128,512]{1,0:T(8,128)(2,1)} %w_one_ref.1, bf16[256,512]{1,0:T(8,128)(2,1)} %w_two_ref.1, f32[1,256]{1,0:T(1,128)} %bitcast.16, f32[1,256]{1,0:T(1,128)} %bitcast.17, ...), custom_call_target="tpu_custom_call" | custom-call | flops 14000000000 | bytes 8388608 | tf_op jit(solution)/shard_map/sage_step/pallas_call | solution.py:467
  127.5 1.6 %copy.22 = bf16[1,256,256]{2,1,0:T(8,128)(2,1)} copy(bf16[1,256,256]{2,1,0:T(8,128)(2,1)} %bitcast.11) | data formatting | bytes 262144
  129.0 1.7 %copy.23 = f32[128,512]{1,0:T(8,128)} copy(f32[128,512]{1,0:T(8,128)} %get-tuple-element.17) | data formatting | bytes 524288
  130.7 1.9 %copy.24 = f32[256,512]{1,0:T(8,128)} copy(f32[256,512]{1,0:T(8,128)} %get-tuple-element.18) | data formatting | bytes 1048576
  132.6 1.2 copy.25

commit v3 on v2

--- a/solution.py
+++ b/solution.py
@@ -6,7 +6,7 @@
 from jax.sharding import PartitionSpec as P
 
 MESH = pl.DeviceIdType.MESH
-CHUNKS = 4
+CHUNKS = (256, 256, 256, 128, 128)
 HALVES = 2
 FEATS = 8
 SIDE = 4
@@ -52,9 +52,9 @@
     z, core = f // 2, f % 2
     u, v = line_place(core, n)
     rows_one = slab.shape[1]
-    rows_two = own_one.shape[0]
-    rows_three = own_two.shape[0]
-    part = rows_one // CHUNKS
+    rows_two = own_one.shape[1]
+    rows_three = own_two.shape[1]
+    starts = [sum(CHUNKS[:c]) for c in range(len(CHUNKS))]
     half = rows_two // HALVES
     slots = [(dz, dc) for dz in range(4) for dc in range(2)]
     by_far = (2, 1, 3)
@@ -109,21 +109,28 @@
     for copy in index_loads:
         copy.wait()
     for own, slo, lower in ((own_one, slo_one, 0), (own_two, slo_two, rows_two)):
-        owner_t = jnp.transpose(own[...].astype(F32))
-        slot_t = jnp.transpose(slo[...].astype(F32))
+        owner_t, slot_t = own[...], slo[...]
         for e in range(SIDE):
             for d in range(SIDE):
                 at = node_at(core, (u - d + SIDE) % SIDE, (v + e) % SIDE)
                 found = jnp.max(
-                    jnp.where(owner_t == at.astype(F32), slot_t, -1.0), axis=0, keepdims=True
+                    jnp.where(owner_t == at, slot_t, -1), axis=0, keepdims=True
                 )
-                asks_out[e, d:d + 1, lower:lower + own.shape[0]] = found.astype(I32)
+                asks_out[e, d:d + 1, lower:lower + own.shape[1]] = found
     for e in range(SIDE):
         asks_out[e, SIDE:] = jnp.full((8 - SIDE, rows_two + rows_three), -1, I32)
     cot_load.wait()
     msg_two[0] = (cot[...] / FAN).astype(BF)
 
     pl.semaphore_wait(barrier, len(partners))
+
+    def send_chunk(c):
+        rows = pl.ds(starts[c], CHUNKS[c])
+        copies = []
+        for i in (4, 5, 2, 3, 6, 7, 1):
+            dev = feat_dev(*slots[i])
+            copies.append(send(feat_ref.at[dev[0], rows], slab.at[i, rows], dev))
+        return copies
 
     low, high = n % SIDE, n // SIDE
     w_copies = []
@@ -135,15 +142,10 @@
                              pl.ds(pl.multiple_of(low * 128, 128), 128)],
                 w_parts.at[i, their_u, their_v], feat_dev(dz, dc),
             ))
+    first_chunk = send_chunk(0)
     ask_copies = [send(asks_out.at[e], asks.at[e], v_dev(e)) for e in range(1, SIDE)]
     msg_two_copies = [send(msg_two.at[0], msg_two.at[e], v_dev(e)) for e in range(1, SIDE)]
-    slab_copies = []
-    for c in range(CHUNKS):
-        rows = pl.ds(c * part, part)
-        slab_copies.append([])
-        for i in (4, 5, 2, 3, 6, 7, 1):
-            dev = feat_dev(*slots[i])
-            slab_copies[c].append(send(feat_ref.at[dev[0], rows], slab.at[i, rows], dev))
+    slab_copies = [first_chunk] + [send_chunk(c) for c in range(1, len(CHUNKS))]
 
     for copy in w_copies:
         copy.wait_recv()
@@ -154,11 +156,6 @@
         copy.wait_recv()
     for e in range(SIDE):
         asks_col[e] = jnp.transpose(asks[e].astype(F32)).astype(I32)
-    for copy in along_u:
-        copy.wait_recv()
-    mine = w_parts.at[pl.ds(1, FEATS - 1), :, v]
-    along_v = [send(mine, mine, v_dev(e)) for e in range(1, SIDE)]
-
     for copy in msg_two_copies:
         copy.wait_recv()
     msgs = jnp.concatenate([msg_two[e] for e in range(SIDE)], axis=0)
@@ -174,6 +171,21 @@
             back_two.append(send(gsend_two.at[d - 1], grecv_two.at[d - 1], u_dev(-d)))
         else:
             gsum_two[...] = total
+
+    for copy in along_u:
+        copy.wait_recv()
+    mine = w_parts.at[pl.ds(1, FEATS - 1), :, v]
+    along_v = [send(mine, mine, v_dev(e)) for e in range(1, SIDE)]
+
+    for copy in back_two:
+        copy.wait_recv()
+    for copy in small_loads:
+        copy.wait()
+    gtab_two = add_up(gsum_two[...], [grecv_two[d] for d in range(SIDE - 1)])
+    gproj_two[:rows_three, :256] = cot[...].astype(BF)
+    gproj_two[rows_three:, :256] = jnp.zeros((rows_two - rows_three, 256), BF)
+    gproj_two[:, 256:] = gtab_two.astype(BF)
+    ghid[...] = dot(gproj_two[...], w_two[...], ((1,), (1,)))
 
     for copy in along_v:
         copy.wait_recv()
@@ -191,7 +203,7 @@
     def project(c):
         for copy in slab_copies[c]:
             copy.wait_recv()
-        lower = c * part
+        lower, part = starts[c], CHUNKS[c]
         block = jnp.concatenate([slab[i, lower:lower + part] for i in range(FEATS)], axis=1)
         table[0, lower:lower + part] = dot(block, w_full[:, 256:]).astype(BF)
         rows = pl.ds(lower, part)
@@ -202,13 +214,14 @@
             self_one[lower:lower + part] = dot(block, w_full[:, :256])
 
     def line_sums(c, e, lower, count):
-        ids = lax.broadcasted_iota(I32, (count, part), 1) + c * part
+        start, part = starts[c], CHUNKS[c]
+        ids = lax.broadcasted_iota(I32, (count, part), 1) + start
         picks = jnp.concatenate(
             [(ids == asks_col[e, lower:lower + count, d:d + 1]).astype(BF)
              for d in range(SIDE)], axis=1
         )
         rows = jnp.concatenate(
-            [table[d, c * part:c * part + part] for d in range(SIDE)], axis=0
+            [table[d, start:start + part] for d in range(SIDE)], axis=0
         )
         return dot(picks, rows)
 
@@ -224,21 +237,11 @@
         lax.fori_loop(0, SIDE, one, 0)
 
     own_load.wait()
-    for c in range(CHUNKS):
+    for c in range(len(CHUNKS)):
         project(c)
         if c:
             add_lines(c - 1)
-        if c == 1:
-            for copy in back_two:
-                copy.wait_recv()
-            for copy in small_loads:
-                copy.wait()
-            gtab_two = add_up(gsum_two[...], [grecv_two[d] for d in range(SIDE - 1)])
-            gproj_two[:rows_three, :256] = cot[...].astype(BF)
-            gproj_two[rows_three:, :256] = jnp.zeros((rows_two - rows_three, 256), BF)
-            gproj_two[:, 256:] = gtab_two.astype(BF)
-            ghid[...] = dot(gproj_two[...], w_two[...], ((1,), (1,)))
-    last = CHUNKS - 1
+    last = len(CHUNKS) - 1
     for copy in table_copies[last]:
         copy.wait_recv()
     y_copies = []
@@ -313,6 +316,16 @@
             return carry
 
         lax.fori_loop(0, SIDE, add_back, 0)
+    for copy in two_copies:
+        copy.wait_recv()
+    for a in range(SIDE):
+        two_mid[a] = add_up(
+            two_out[a, v].astype(F32), [two_in[e, a] for e in range(SIDE - 1)]
+        ).astype(BF)
+    two_copies = [
+        send(two_mid.at[(u + d) % SIDE], two_u.at[d - 1], u_dev(d)) for d in by_far
+    ]
+
     for copy in msg_copies[HALVES - 1]:
         copy.wait_recv()
     back_one = []
@@ -326,13 +339,8 @@
 
     for copy in two_copies:
         copy.wait_recv()
-    for a in range(SIDE):
-        two_mid[a] = add_up(
-            two_out[a, v].astype(F32), [two_in[e, a] for e in range(SIDE - 1)]
-        ).astype(BF)
-    two_copies = [
-        send(two_mid.at[(u + d) % SIDE], two_u.at[d - 1], u_dev(d)) for d in by_far
-    ]
+    two_z[0] = add_up(two_mid[u].astype(F32), [two_u[d] for d in range(SIDE - 1)]).astype(BF)
+    two_copies = [send(two_z.at[0], two_z.at[i], feat_dev(*slots[i])) for i in range(1, FEATS)]
 
     for copy in table_two_copies:
         copy.wait_recv()
@@ -352,20 +360,19 @@
 
     for copy in two_copies:
         copy.wait_recv()
-    two_z[0] = add_up(two_mid[u].astype(F32), [two_u[d] for d in range(SIDE - 1)]).astype(BF)
-    two_copies = [send(two_z.at[0], two_z.at[i], feat_dev(*slots[i])) for i in range(1, FEATS)]
-
-    for copy in y_two:
-        copy.wait_recv()
-    total = add_up(ysum_two[...], [yrecv_two[e] for e in range(SIDE - 1)])
-    out_ref[...] = (self_two[...] + b_two[...] + total / FAN).astype(BF)
-
-    for copy in two_copies:
-        copy.wait_recv()
     two_all[u, v] = add_up(
         two_z[0].astype(F32), [two_z[i] for i in range(1, FEATS)]
     ).astype(BF)
     two_copies = [send(two_all.at[u, v], two_all.at[u, v], v_dev(e)) for e in by_far]
+
+    for copy in y_two:
+        copy.wait_recv()
+    total = add_up(ysum_two[...], [yrecv_two[e] for e in range(SIDE - 1)])
+    out_ref[...] = (self_two[...] + b_two[...] + total / FAN).astype(BF)
+
+    for copy in two_copies:
+        copy.wait_recv()
+    two_copies = [send(two_all.at[u], two_all.at[u], u_dev(d)) for d in by_far]
 
     for copy in back_one:
         copy.wait_recv()
@@ -381,9 +388,6 @@
     pair_out[:, 256:] = right.astype(BF)
     pair = send(pair_out, pair_in, feat_dev(0, 1))
     left, right = outer(0)
-    for copy in two_copies:
-        copy.wait_recv()
-    two_copies = [send(two_all.at[u], two_all.at[u], u_dev(d)) for d in by_far]
     pair.wait_recv()
     left = (left + pair_in[:, :256].astype(F32)).astype(BF)
     right = (right + pair_in[:, 256:].astype(F32)).astype(BF)
@@ -438,7 +442,7 @@
         copy.wait_send()
 
 
-N_COPIES = 7 * (3 + CHUNKS) + 3 * (CHUNKS + 2 * HALVES) + 3 * 18
+N_COPIES = 7 * (3 + len(CHUNKS)) + 3 * (len(CHUNKS) + 2 * HALVES) + 3 * 18
 
 
 def on_device(
@@ -449,7 +453,7 @@
     scratch = [
         ((FEATS, r1, 128), BF), ((FEATS, 4, 4, 32, 128), BF), ((1024, 512), BF),
         ((256, 512), BF), ((1, 256), F32), ((1, 256), F32),
-        ((r2, FAN), I32), ((r2, FAN), I32), ((r3, FAN), I32), ((r3, FAN), I32),
+        ((FAN, r2), I32), ((FAN, r2), I32), ((FAN, r3), I32), ((FAN, r3), I32),
         ((r3, 256), F32), ((SIDE, 8, r2 + r3), I32),
         ((SIDE, 8, r2 + r3), I32), ((SIDE, r2 + r3, 8), I32),
         ((SIDE, r3, 256), BF), ((r2, 256), F32), ((3, r2, 256), BF), ((3, r2, 256), BF),
@@ -470,21 +474,21 @@
             jax.ShapeDtypeStruct((r3, 256), BF), jax.ShapeDtypeStruct((128, 512), F32),
             jax.ShapeDtypeStruct((256, 512), F32), jax.ShapeDtypeStruct((1, 256), F32),
         ],
-        in_specs=[pl.BlockSpec(memory_space=pl.ANY)] * 10,
+        in_specs=[pl.BlockSpec(memory_space=pltpu.HBM)] * 10,
         out_specs=[vm] * 4,
         scratch_shapes=[pltpu.VMEM(s, t) for s, t in scratch] + [
             pltpu.SemaphoreType.DMA((N_COPIES,)), pltpu.SemaphoreType.DMA((N_COPIES,)),
             pltpu.SemaphoreType.DMA((10,)),
         ],
         compiler_params=pltpu.CompilerParams(
-            collective_id=0, has_side_effects=True, vmem_limit_bytes=56 * 2**20
+            collective_id=0, has_side_effects=True, vmem_limit_bytes=36 * 2**20
         ),
         cost_estimate=pl.CostEstimate(
             flops=14 * 10**9, bytes_accessed=8 * 2**20, transcendentals=512 * 256
         ),
         name="sage_step",
-    )(features, w_one, w_two, b_one[None], b_two[None], owner_one[0], slot_one[0],
-      owner_two[0], slot_two[0], cotangent[0])
+    )(features, w_one, w_two, b_one[None], b_two[None], owner_one[0].T, slot_one[0].T,
+      owner_two[0].T, slot_two[0].T, cotangent[0])
     return layer_out[None], gw_one, gw_two, gb[0]
 
 

time: 135 us -> 135 us (level)
    pallas_call x1, Pallas kernels: 121 us -> 122 us  [on_device(): pl.pallas_call(step_kernel, out_shape=[jax.ShapeDtypeStruct((r3, 256), BF...]
    unnamed x8 -> x24, local copies, waits for them, and re-layouts: 12.4 us -> 11.3 us
where the time goes in v3:
time: 135 us; the launch traced here: 134 us
  Pallas kernels  122 us (90%)
  local copies, waits for them, and re-layouts  11.3 us (8%)
    pallas_call x1, Pallas kernels, on_device(): pl.pallas_call(step_kernel, out_shape=[jax.ShapeDtypeStruct((r3, 256), BF...  122 us
    unnamed x24, local copies, waits for them, and re-layouts  11.3 us

profile of v3, /device:TPU:0, one launch (start us, length us, event | category | flops | bytes accessed | tf_op | source)
XLA Modules:
  0.0 134.3 jit_solution(1798044975140774533)
XLA Ops:
  0.6 0.0 copy-start
  0.6 1.6 %copy-done = bf16[8,1024,128]{2,1,0:T(8,128)(2,1)S(1)} copy-done((bf16[8,1024,128]{2,1,0:T(8,128)(2,1)S(1)}, bf16[8,1024,128]{2,1,0:T(8,128)(2,1)}, u32[]{:S(2)}) %copy-start) | copy-done | bytes 2097176
  2.2 0.0 copy-start.1
  2.2 0.9 copy-done.1
  3.2 0.0 copy-start.2
  3.2 0.9 copy-done.2
  4.1 0.0 copy-start.3
  4.1 0.9 copy-done.3
  5.0 0.0 copy-start.4
  5.0 0.7 copy-done.4
  5.8 0.0 copy-start.5
  5.8 0.7 copy-done.5
  6.5 0.0 copy-start.6
  6.5 0.7 copy-done.6
  7.2 0.0 copy-start.7
  7.2 0.7 copy-done.7
  7.9 0.0 copy-start.8
  7.9 0.7 copy-done.8
  8.5 0.7 copy-done.9
  9.2 122.4 %sage_step.1 = (bf16[256,256]{1,0:T(8,128)(2,1)S(1)}, f32[128,512]{1,0:T(8,128)S(1)}, f32[256,512]{1,0:T(8,128)S(1)}, f32[1,256]{1,0:T(1,128)S(1)}) custom-call(bf16[8,1024,128]{2,1,0:T(8,128)(2,1)S(1)} %copy-done, bf16[128,512]{1,0:T(8,128)(2,1)S(1)} %copy-done.3, bf16[256,512]{1,0:T(8,128)(2,1)S(1)} %copy-done.1, f32[1,256]{1,0:T(1,128)S(1)} %bitcast.24, ...), custom_call_target="tpu_custom_call" | custom-call | flops 14000000000 | bytes 8388608 | tf_op jit(solution)/shard_map/sage_step/pallas_call | solution.py:471
  131.6 0.7 copy.18
  132.3 0.7 copy.19
  133.0 0.8 copy.20
  133.8 0.6 copy.21
  (1 shorter events, 0.0 us)
Async XLA Ops:
  0.6 1.6 %copy-start = (bf16[8,1024,128]{2,1,0:T(8,128)(2,1)S(1)}, bf16[8,1024,128]{2,1,0:T(8,128)(2,1)}, u32[]{:S(2)}) copy-start(bf16[8,1024,128]{2,1,0:T(8,128)(2,1)} %feat_ref.1) | copy-start | bytes 6291460
  2.2 0.9 copy-start.1
  3.2 0.9 copy-start.2
  4.1 0.9 copy-start.3
  5.0 0.7 copy-start.4
  5.8 0.7 copy-start.5
  6.5 0.7 copy-start.6
  7.2 0.7 copy-start.7
  7.9 0.7 copy-start.8
  8.5 0.7 copy-start.9

commit v4 on v3

v4 whole, which is shorter than its diff:
```python
import jax
import jax.numpy as jnp
from jax import lax
from jax.experimental import pallas as pl
from jax.experimental.pallas import tpu as pltpu
from jax.sharding import PartitionSpec as P

MESH = pl.DeviceIdType.MESH
PART = 256
FEATS = 8
SIDE = 4
FAN = 8
BF = jnp.bfloat16
F32 = jnp.float32
I32 = jnp.int32


def line_place(core, node):
    low, high = node % SIDE, node // SIDE
    return (1 - core) * low + core * high, (1 - core) * high + core * low


def node_at(core, u, v):
    return (1 - core) * (v * SIDE + u) + core * (u * SIDE + v)


def dot(a, b, dims=((1,), (0,))):
    return lax.dot_general(a, b, (dims, ((), ())), preferred_element_type=F32)


def add_up(first, others):
    total = first
    for other in others:
        total += other.astype(F32)
    return total


def step_kernel(
    feat_ref, w_one_ref, w_two_ref, b_one_ref, b_two_ref, owner_one_ref, slot_one_ref,
    owner_two_ref, slot_two_ref, cot_ref,
    out_ref, gw_one_ref, gw_two_ref, gb_ref,
    slab, w_parts, w_full, w_two, b_one, b_two, own_one, slo_one, own_two, slo_two, cot,
    asks_out, asks, asks_col, msg_two, gsum_two, gsend_two, grecv_two,
    gproj_two, ghid, table, self_one, ysum, ysend, yrecv, hidden, self_two,
    table_two, ysum_two, ysend_two, yrecv_two, glin, msg_one, gsum, gsend, grecv, bias,
    two_out, two_in, two_mid, two_v, two_z, two_all,
    wall, gtab, pair_out, pair_in, w_out, w_in, w_mid, v_in, z_out, z_in, piece_all,
    ssem, rsem, lsem,
):
    f, n = lax.axis_index("feat"), lax.axis_index("node")
    z, core = f // 2, f % 2
    u, v = line_place(core, n)
    rows_one = slab.shape[1]
    rows_two = own_one.shape[1]
    rows_three = own_two.shape[1]
    chunks = rows_one // PART
    tiles = rows_two // PART
    slots = [(dz, dc) for dz in range(4) for dc in range(2)]
    others = (2, 1, 3)

    def feat_dev(dz, dc):
        return (((z + dz + 4) % 4) * 2 + (core + dc) % 2, n)

    def u_dev(d):
        return (f, node_at(core, (u + d + SIDE) % SIDE, v))

    def v_dev(e):
        return (f, node_at(core, u, (v + e + SIDE) % SIDE))

    def place(r, q):
        return (1 - core) * q + core * r, (1 - core) * r + core * q

    def tile(j, size=PART):
        return pl.ds(pl.multiple_of(j * size, size), size)

    used = [0]
    groups = []

    def group(count):
        first = used[0]
        used[0] += count
        return first

    def describe(k, src, dst, dev):
        return pltpu.make_async_remote_copy(
            src_ref=src, dst_ref=dst, send_sem=ssem.at[k], recv_sem=rsem.at[k],
            device_id=dev, device_id_type=MESH,
        )

    def send(src, dst, dev):
        copy = describe(group(1), src, dst, dev)
        copy.start()
        groups.append(copy)
        return copy

    def arrived(copies):
        for copy in copies:
            copy.wait_recv()

    barrier = pltpu.get_barrier_semaphore()
    partners = [feat_dev(*s) for s in slots[1:]]
    partners += [u_dev(d) for d in range(1, SIDE)] + [v_dev(e) for e in range(1, SIDE)]
    for dev in partners:
        pl.semaphore_signal(barrier, inc=1, device_id=dev, device_id_type=MESH)

    loads = []

    def load(src, dst):
        copy = pltpu.make_async_copy(src, dst, lsem.at[len(loads)])
        copy.start()
        loads.append(copy)
        return copy

    index_loads = [
        load(owner_one_ref, own_one), load(slot_one_ref, slo_one),
        load(owner_two_ref, own_two), load(slot_two_ref, slo_two),
    ]
    cot_load = load(cot_ref, cot)
    w_one_load = load(w_one_ref, w_full.at[pl.ds(0, 128)])
    own_load = load(feat_ref.at[f], slab.at[0])
    small_loads = [load(w_two_ref, w_two), load(b_one_ref, b_one), load(b_two_ref, b_two)]

    for copy in index_loads:
        copy.wait()

    def ask_line(e, carry):
        for own, slo, lower in ((own_one, slo_one, 0), (own_two, slo_two, rows_two)):
            owner, slot = own[...], slo[...]
            found = []
            for d in range(SIDE):
                at = node_at(core, (u - d + SIDE) % SIDE, (v + e) % SIDE)
                found.append(jnp.max(jnp.where(owner == at, slot, -1), axis=0, keepdims=True))
            found.append(jnp.full((8 - SIDE, own.shape[1]), -1, I32))
            asks_out[e, :, lower:lower + own.shape[1]] = jnp.concatenate(found, axis=0)
        return carry

    lax.fori_loop(0, SIDE, ask_line, 0)
    cot_load.wait()
    msg_two[0] = (cot[...] / FAN).astype(BF)

    def clear(j, carry):
        ysum[j] = jnp.zeros((rows_two, 256), F32)
        gsum[j] = jnp.zeros((rows_one, 256), F32)
        return carry

    lax.fori_loop(0, SIDE, clear, 0)
    bias[...] = jnp.zeros((1, 256), F32)

    pl.semaphore_wait(barrier, len(partners))

    low, high = n % SIDE, n // SIDE
    w_copies = []
    for i, (dz, dc) in enumerate(slots):
        if i:
            their_u, their_v = line_place((core + dc) % 2, n)
            w_copies.append(send(
                w_one_ref.at[pl.ds(pl.multiple_of(high * 32, 32), 32),
                             pl.ds(pl.multiple_of(low * 128, 128), 128)],
                w_parts.at[i, their_u, their_v], feat_dev(dz, dc),
            ))
    slab_at = group(7 * chunks)

    def slab_copy(c, i):
        dev = feat_dev(*slots[i])
        return describe(slab_at + c * 7 + i - 1, feat_ref.at[dev[0], tile(c)],
                        slab.at[i, tile(c)], dev)

    def send_chunk(c, carry):
        for i in (4, 5, 2, 3, 6, 7, 1):
            slab_copy(c, i).start()
        return carry

    send_chunk(0, 0)
    ask_copies = [send(asks_out.at[e], asks.at[e], v_dev(e)) for e in range(1, SIDE)]
    msg_two_copies = [send(msg_two.at[0], msg_two.at[e], v_dev(e)) for e in range(1, SIDE)]
    lax.fori_loop(1, chunks, send_chunk, 0)

    arrived(w_copies)
    mine = w_parts.at[pl.ds(1, FEATS - 1), u, v]
    along_u = [send(mine, mine, u_dev(d)) for d in range(1, SIDE)]
    asks[0] = asks_out[0]
    arrived(ask_copies)

    def turn(e, carry):
        asks_col[e] = jnp.transpose(asks[e].astype(F32)).astype(I32)
        return carry

    lax.fori_loop(0, SIDE, turn, 0)

    arrived(msg_two_copies)
    back_two_at = group(3 * tiles)

    def back_two(d, t):
        return describe(back_two_at + (d - 1) * tiles + t, gsend_two.at[d - 1, tile(t)],
                        grecv_two.at[d - 1, tile(t)], u_dev(-d))

    def back_two_step(j, carry):
        d, t = (j // tiles + 1) % SIDE, j % tiles
        ids = lax.broadcasted_iota(I32, (PART, rows_three), 0) + t * PART
        picks = jnp.concatenate(
            [(ids == asks[e, pl.ds(d, 1), rows_two:]).astype(BF) for e in range(SIDE)], axis=1
        )
        value = dot(picks, jnp.concatenate([msg_two[e] for e in range(SIDE)], axis=0))

        @pl.when(d > 0)
        def _():
            gsend_two[d - 1, tile(t)] = value.astype(BF)
            back_two(d, t).start()

        @pl.when(d == 0)
        def _():
            gsum_two[tile(t)] = value

        return carry

    lax.fori_loop(0, SIDE * tiles, back_two_step, 0)
    arrived(along_u)
    mine = w_parts.at[pl.ds(1, FEATS - 1), :, v]
    along_v = [send(mine, mine, v_dev(e)) for e in range(1, SIDE)]

    for copy in small_loads:
        copy.wait()
    arrived([back_two(d, t) for d in range(1, SIDE) for t in range(tiles)])
    gproj_two[:rows_three, :256] = cot[...].astype(BF)
    gproj_two[rows_three:, :256] = jnp.zeros((rows_two - rows_three, 256), BF)

    def ghid_step(t, carry):
        total = add_up(gsum_two[tile(t, 128)], [grecv_two[d, tile(t, 128)] for d in range(3)])
        gproj_two[tile(t, 128), 256:] = total.astype(BF)
        ghid[tile(t, 128)] = dot(gproj_two[tile(t, 128)], w_two[...], ((1,), (1,)))
        return carry

    lax.fori_loop(0, rows_two // 128, ghid_step, 0)

    arrived(along_v)
    w_one_load.wait()

    def lay_w(i, carry):
        for r in range(4):
            for q in range(4):
                a, b = place(r, q)
                w_full[pl.ds(pl.multiple_of(i * 128 + r * 32, 32), 32),
                       q * 128:q * 128 + 128] = w_parts[i, a, b]
        return carry

    lax.fori_loop(1, FEATS, lay_w, 0)
    own_load.wait()

    table_at = group(3 * chunks)
    y_at = group(3 * tiles)

    def table_copy(c, d):
        return describe(table_at + c * 3 + d - 1, table.at[0, tile(c)], table.at[d, tile(c)],
                        u_dev(d))

    def y_copy(e, h):
        return describe(y_at + h * 3 + e - 1, ysend.at[e - 1, tile(h)], yrecv.at[e - 1, tile(h)],
                        v_dev(-e))

    def chunk_step(c, carry):
        @pl.when(c < chunks)
        def _():
            arrived([slab_copy(c, i) for i in range(1, FEATS)])
            block = jnp.concatenate([slab[i, tile(c)] for i in range(FEATS)], axis=1)
            table[0, tile(c)] = dot(block, w_full[:, 256:]).astype(BF)
            for d in others:
                table_copy(c, d).start()

            @pl.when(c < tiles)
            def _():
                self_one[tile(c)] = dot(block, w_full[:, :256])

        @pl.when(c > 0)
        def _():
            arrived([table_copy(c - 1, d) for d in others])

            def sum_step(j, inner):
                h, e = j // SIDE, (j + 1) % SIDE
                ids = lax.broadcasted_iota(I32, (PART, PART), 1) + (c - 1) * PART
                picks = jnp.concatenate(
                    [(ids == asks_col[e, tile(h), d:d + 1]).astype(BF) for d in range(SIDE)],
                    axis=1,
                )
                rows = jnp.concatenate([table[d, tile(c - 1)] for d in range(SIDE)], axis=0)
                value = ysum[e, tile(h)] + dot(picks, rows)
                ysum[e, tile(h)] = value

                @pl.when((c == chunks) & (e > 0))
                def _():
                    ysend[e - 1, tile(h)] = value.astype(BF)
                    y_copy(e, h).start()

                return inner

            lax.fori_loop(0, SIDE * tiles, sum_step, 0)

        return carry

    lax.fori_loop(0, chunks + 1, chunk_step, 0)

    msg_at = group(3 * tiles)

    def msg_copy(h, e):
        return describe(msg_at + h * 3 + e - 1, msg_one.at[0, tile(h)], msg_one.at[e, tile(h)],
                        v_dev(e))

    def act_step(h, carry):
        arrived([y_copy(e, h) for e in others])

        def rows_step(t, inner):
            rows = pl.ds(pl.multiple_of(h * PART + t * 64, 64), 64)
            total = add_up(ysum[0, rows], [yrecv[e, rows] for e in range(SIDE - 1)])
            linear = self_one[rows] + b_one[...] + total / FAN
            logistic = 1.0 / (1.0 + jnp.exp(-linear))
            grad = ghid[rows] * (logistic * (1.0 + linear * (1.0 - logistic)))
            msg_one[0, rows] = (grad / FAN).astype(BF)
            glin[rows] = grad.astype(BF)
            hidden[rows] = (linear * logistic).astype(BF)
            bias[...] += jnp.sum(grad, axis=0, keepdims=True)
            return inner

        lax.fori_loop(0, PART // 64, rows_step, 0)
        for e in others:
            msg_copy(h, e).start()
        return carry

    lax.fori_loop(0, tiles, act_step, 0)

    def gw_two_step(k, carry):
        value = dot(hidden[:, tile(k, 128)], gproj_two[...], ((0,), (0,))).astype(BF)
        for r in range(2):
            for q in range(4):
                a, b = place(2 * k + r, q)
                two_out[a, b, :64] = value[r * 64:r * 64 + 64, q * 128:q * 128 + 128]
                two_out[a, b, 64:] = jnp.zeros((16, 128), BF)
        return carry

    lax.fori_loop(0, 2, gw_two_step, 0)
    for q in range(2):
        a, b = place(0, q)
        two_out[a, b, 64:] = jnp.broadcast_to(bias[:, q * 128:q * 128 + 128], (16, 128)).astype(BF)
    two_u_copies = [
        send(two_out.at[(u + d) % SIDE], two_in.at[d - 1], u_dev(d)) for d in others
    ]

    def proj_two_step(t, carry):
        proj = dot(hidden[tile(t, 128)], w_two[...])
        table_two[0, tile(t, 128)] = proj[:, 256:].astype(BF)

        @pl.when(t < rows_three // 128)
        def _():
            self_two[tile(t, 128)] = proj[:, :256]

        return carry

    lax.fori_loop(0, rows_two // 128, proj_two_step, 0)
    table_two_copies = [send(table_two.at[0], table_two.at[d], u_dev(d)) for d in others]

    two_v_at = group(3)
    back_at = group(3 * chunks)

    def two_v_copy(e):
        return describe(two_v_at + e - 1, two_mid.at[(v + e) % SIDE], two_v.at[e - 1], v_dev(e))

    def back_copy(d, t):
        return describe(back_at + (d - 1) * chunks + t, gsend.at[d - 1, tile(t)],
                        grecv.at[d - 1, tile(t)], u_dev(-d))

    def back_step(h, carry):
        @pl.when(h == tiles - 1)
        def _():
            arrived(two_u_copies)
            for b in range(SIDE):
                two_mid[b] = add_up(
                    two_out[u, b].astype(F32), [two_in[d, b] for d in range(SIDE - 1)]
                ).astype(BF)
            for e in others:
                two_v_copy(e).start()

        arrived([msg_copy(h, e) for e in others])

        def grad_step(j, inner):
            d, t = (j // chunks + 1) % SIDE, j % chunks
            ids = lax.broadcasted_iota(I32, (PART, PART), 0) + t * PART
            picks = jnp.concatenate(
                [(ids == asks[e, pl.ds(d, 1), tile(h)]).astype(BF) for e in range(SIDE)], axis=1
            )
            rows = jnp.concatenate([msg_one[e, tile(h)] for e in range(SIDE)], axis=0)
            value = gsum[d, tile(t)] + dot(picks, rows)
            gsum[d, tile(t)] = value

            @pl.when((h == tiles - 1) & (d > 0))
            def _():
                gsend[d - 1, tile(t)] = value.astype(BF)
                back_copy(d, t).start()

            return inner

        lax.fori_loop(0, SIDE * chunks, grad_step, 0)
        return carry

    lax.fori_loop(0, tiles, back_step, 0)
    arrived([two_v_copy(e) for e in others])
    two_z[0] = add_up(two_mid[v].astype(F32), [two_v[e] for e in range(SIDE - 1)]).astype(BF)
    two_z_copies = [
        send(two_z.at[0], two_z.at[i], feat_dev(*slots[i])) for i in range(1, FEATS)
    ]

    arrived(table_two_copies)
    y_two_at = group(6)

    def y_two_copy(e, h):
        return describe(y_two_at + h * 3 + e - 1, ysend_two.at[e - 1, tile(h, 128)],
                        yrecv_two.at[e - 1, tile(h, 128)], v_dev(-e))

    def y_two_step(j, carry):
        e, h = (j // 2 + 1) % SIDE, j % 2
        ids = lax.broadcasted_iota(I32, (128, rows_two), 1)
        lower = pl.ds(pl.multiple_of(rows_two + h * 128, 128), 128)
        picks = jnp.concatenate(
            [(ids == asks_col[e, lower, d:d + 1]).astype(BF) for d in range(SIDE)], axis=1
        )
        value = dot(picks, jnp.concatenate([table_two[d] for d in range(SIDE)], axis=0))

        @pl.when(e > 0)
        def _():
            ysend_two[e - 1, tile(h, 128)] = value.astype(BF)
            y_two_copy(e, h).start()

        @pl.when(e == 0)
        def _():
            ysum_two[tile(h, 128)] = value

        return carry

    lax.fori_loop(0, 2 * SIDE, y_two_step, 0)

    arrived(two_z_copies)
    two_all[u, v] = add_up(
        two_z[0].astype(F32), [two_z[i] for i in range(1, FEATS)]
    ).astype(BF)
    two_copies = [send(two_all.at[u, v], two_all.at[u, v], v_dev(e)) for e in others]
    arrived([y_two_copy(e, h) for e in others for h in range(2)])

    def out_step(t, carry):
        total = add_up(ysum_two[tile(t, 64)], [yrecv_two[e, tile(t, 64)] for e in range(3)])
        out_ref[tile(t, 64)] = (self_two[tile(t, 64)] + b_two[...] + total / FAN).astype(BF)
        return carry

    lax.fori_loop(0, rows_three // 64, out_step, 0)
    arrived(two_copies)
    two_copies = [send(two_all.at[u], two_all.at[u], u_dev(d)) for d in others]

    arrived([back_copy(d, t) for d in others for t in range(chunks)])

    def gtab_step(t, carry):
        gtab[tile(t, 128)] = add_up(
            gsum[0, tile(t, 128)], [grecv[d, tile(t, 128)] for d in range(SIDE - 1)]
        ).astype(BF)
        return carry

    lax.fori_loop(0, rows_one // 128, gtab_step, 0)
    pair_at = group(1)
    pair = describe(pair_at, pair_out, pair_in, feat_dev(0, 1))

    def outer_step(k, carry):
        block = slab[2 * (k % 4) + 1 - k // 4]
        wall[k, :, :256] = dot(block[:rows_two], glin[...], ((0,), (0,)))
        wall[k, :, 256:] = dot(block, gtab[...], ((0,), (0,)))

        @pl.when(k < 4)
        def _():
            pair_out[k] = wall[k].astype(BF)

        @pl.when(k == 3)
        def _():
            pair.start()

        return carry

    lax.fori_loop(0, FEATS, outer_step, 0)
    pair.wait_recv()

    def piece_step(dz, carry):
        value = (wall[4 + dz] + pair_in[dz].astype(F32)).astype(BF)
        for r in range(4):
            for q in range(4):
                a, b = place(r, q)
                w_out[a, b, tile(dz, 32)] = value[r * 32:r * 32 + 32, q * 128:q * 128 + 128]
        return carry

    lax.fori_loop(0, 4, piece_step, 0)

    sums = [send(w_out.at[(u + d) % SIDE], w_in.at[d - 1], u_dev(d)) for d in others]
    arrived(two_copies)

    def lay_two(r, carry):
        for q in range(4):
            a, b = place(r, q)
            gw_two_ref[tile(r, 64), q * 128:q * 128 + 128] = two_all[a, b, :64].astype(F32)
        return carry

    lax.fori_loop(0, 4, lay_two, 0)
    for q in range(2):
        a, b = place(0, q)
        gb_ref[:, q * 128:q * 128 + 128] = two_all[a, b, 64:].astype(F32)[:1]
    arrived(sums)

    def mid_step(b, carry):
        w_mid[b] = add_up(
            w_out[u, b].astype(F32), [w_in[d, b] for d in range(SIDE - 1)]
        ).astype(BF)
        return carry

    lax.fori_loop(0, SIDE, mid_step, 0)
    sums = [send(w_mid.at[(v + e) % SIDE], v_in.at[e - 1], v_dev(e)) for e in others]
    arrived(sums)
    z_out[...] = add_up(w_mid[v].astype(F32), [v_in[e] for e in range(SIDE - 1)]).astype(BF)
    sums = [
        send(z_out.at[pl.ds(dz * 32, 32)], z_in.at[dz - 1], feat_dev(-dz, 0)) for dz in others
    ]
    arrived(sums)
    piece_all[u, v] = add_up(
        z_out[:32].astype(F32), [z_in[dz] for dz in range(3)]
    ).astype(BF)
    sums = [send(piece_all.at[u, v], piece_all.at[u, v], v_dev(e)) for e in others]
    arrived(sums)
    sums = [send(piece_all.at[u], piece_all.at[u], u_dev(d)) for d in others]
    arrived(sums)

    def lay_one(r, carry):
        for q in range(4):
            a, b = place(r, q)
            gw_one_ref[tile(r, 32), q * 128:q * 128 + 128] = piece_all[a, b].astype(F32)
        return carry

    lax.fori_loop(0, 4, lay_one, 0)
    for copy in groups:
        copy.wait_send()
    pair.wait_send()

    def sent(c, carry):
        for i in range(1, FEATS):
            slab_copy(c, i).wait_send()
        for d in others:
            table_copy(c, d).wait_send()
            back_copy(d, c).wait_send()
        return carry

    lax.fori_loop(0, chunks, sent, 0)

    def sent_tiles(t, carry):
        for d in others:
            back_two(d, t).wait_send()
            y_copy(d, t).wait_send()
            msg_copy(t, d).wait_send()
        return carry

    lax.fori_loop(0, tiles, sent_tiles, 0)
    for e in others:
        two_v_copy(e).wait_send()
        for h in range(2):
            y_two_copy(e, h).wait_send()


def store_kernel(*refs):
    count = len(refs) // 2
    copies = [
        pltpu.make_async_copy(refs[i], refs[count + i], refs[-1].at[i]) for i in range(count)
    ]
    for copy in copies:
        copy.start()
    for copy in copies:
        copy.wait()


N_COPIES = 160


def on_device(
    features, w_one, w_two, b_one, b_two, owner_one, slot_one, owner_two, slot_two, cotangent
):
    r1, r2, r3 = features.shape[1], owner_one.shape[1], owner_two.shape[1]
    vm = pl.BlockSpec(memory_space=pltpu.VMEM)
    scratch = [
        ((FEATS, r1, 128), BF), ((FEATS, 4, 4, 32, 128), BF), ((1024, 512), BF),
        ((256, 512), BF), ((1, 256), F32), ((1, 256), F32),
        ((FAN, r2), I32), ((FAN, r2), I32), ((FAN, r3), I32), ((FAN, r3), I32),
        ((r3, 256), F32), ((SIDE, 8, r2 + r3), I32),
        ((SIDE, 8, r2 + r3), I32), ((SIDE, r2 + r3, 8), I32),
        ((SIDE, r3, 256), BF), ((r2, 256), F32), ((3, r2, 256), BF), ((3, r2, 256), BF),
        ((r2, 512), BF), ((r2, 256), F32), ((SIDE, r1, 256), BF), ((r2, 256), F32),
        ((SIDE, r2, 256), F32), ((3, r2, 256), BF), ((3, r2, 256), BF), ((r2, 256), BF),
        ((r3, 256), F32), ((SIDE, r2, 256), BF), ((r3, 256), F32), ((3, r3, 256), BF),
        ((3, r3, 256), BF), ((r2, 256), BF), ((SIDE, r2, 256), BF), ((SIDE, r1, 256), F32),
        ((3, r1, 256), BF), ((3, r1, 256), BF), ((1, 256), F32),
        ((4, 4, 80, 128), BF), ((3, 4, 80, 128), BF), ((4, 80, 128), BF), ((3, 80, 128), BF),
        ((FEATS, 80, 128), BF), ((4, 4, 80, 128), BF),
        ((FEATS, 128, 512), F32), ((r1, 256), BF), ((4, 128, 512), BF), ((4, 128, 512), BF),
        ((4, 4, 128, 128), BF), ((3, 4, 128, 128), BF),
        ((4, 128, 128), BF), ((3, 128, 128), BF), ((128, 128), BF), ((3, 32, 128), BF),
        ((4, 4, 32, 128), BF),
    ]
    outs = pl.pallas_call(
        step_kernel,
        out_shape=[
            jax.ShapeDtypeStruct((r3, 256), BF), jax.ShapeDtypeStruct((128, 512), F32),
            jax.ShapeDtypeStruct((256, 512), F32), jax.ShapeDtypeStruct((1, 256), F32),
        ],
        in_specs=[pl.BlockSpec(memory_space=pl.ANY)] * 10,
        out_specs=[vm] * 4,
        scratch_shapes=[pltpu.VMEM(s, t) for s, t in scratch] + [
            pltpu.SemaphoreType.DMA((N_COPIES,)), pltpu.SemaphoreType.DMA((N_COPIES,)),
            pltpu.SemaphoreType.DMA((10,)),
        ],
        compiler_params=pltpu.CompilerParams(
            collective_id=0, has_side_effects=True, vmem_limit_bytes=56 * 2**20
        ),
        cost_estimate=pl.CostEstimate(
            flops=14 * 10**9, bytes_accessed=8 * 2**20, transcendentals=512 * 256
        ),
        name="sage_step",
    )(features, w_one, w_two, b_one[None], b_two[None], owner_one[0].T, slot_one[0].T,
      owner_two[0].T, slot_two[0].T, cotangent[0])
    hbm = pl.BlockSpec(memory_space=pl.ANY)
    layer_out, gw_one, gw_two, gb = pl.pallas_call(
        store_kernel,
        out_shape=[jax.ShapeDtypeStruct(o.shape, o.dtype) for o in outs],
        in_specs=[hbm] * 4,
        out_specs=[hbm] * 4,
        scratch_shapes=[pltpu.SemaphoreType.DMA((4,))],
        compiler_params=pltpu.CompilerParams(vmem_limit_bytes=60 * 2**20),
        name="store_results",
    )(*outs)
    return layer_out[None], gw_one, gw_two, gb[0]


def solution(mesh):
    placed = (
        P(None, "node", "feat"),
        P("feat", None),
        P(),
        P(),
        P(),
        P("feat", "node", None),
        P("feat", "node", None),
        P("feat", "node", None),
        P("feat", "node", None),
        P("feat", "node", None),
    )
    return jax.shard_map(
        on_device,
        mesh=mesh,
        in_specs=placed,
        out_specs=(P("feat", "node", None), P("feat", None), P(), P()),
        check_vma=False,
    )
```

time: 135 us -> 151 us (1.12)
  Pallas kernels: 122 us -> 150 us
  local copies, waits for them, and re-layouts: 11.3 us -> 0 us
    pallas_call x0 -> x1, Pallas kernels: none -> 29 us  [on_device(): pl.pallas_call(store_kernel, out_shape=[jax.ShapeDtypeStruct(o.shape, o.d...]
    unnamed x24 -> x0, local copies, waits for them, and re-layouts: 11.3 us -> none
where the time goes in v4:
time: 151 us
  Pallas kernels  150 us (99%)
    pallas_call x1, Pallas kernels, on_device(): pl.pallas_call(step_kernel, out_shape=[jax.ShapeDtypeStruct((r3, 256), BF...  121 us
    pallas_call x1, Pallas kernels, on_device(): pl.pallas_call(store_kernel, out_shape=[jax.ShapeDtypeStruct(o.shape, o.d...  29 us

profile of v4, /device:TPU:0, one launch (start us, length us, event | category | flops | bytes accessed | tf_op | source)
XLA Modules:
  0.0 150.9 jit_solution(7017429298147954302)
XLA Ops:
  0.6 121.3 %sage_step.1 = (bf16[256,256]{1,0:T(8,128)(2,1)}, f32[128,512]{1,0:T(8,128)}, f32[256,512]{1,0:T(8,128)}, f32[1,256]{1,0:T(1,128)}) custom-call(bf16[8,1024,128]{2,1,0:T(8,128)(2,1)} %feat_ref.1, bf16[128,512]{1,0:T(8,128)(2,1)} %w_one_ref.1, bf16[256,512]{1,0:T(8,128)(2,1)} %w_two_ref.1, f32[1,256]{1,0:T(1,128)} %bitcast.23, f32[1,256]{1,0:T(1,128)} %bitcast.24, ...), custom_call_target="tpu_custom_call" | custom-call | flops 14000000000 | bytes 8388608 | tf_op jit(solution)/shard_map/sage_step/pallas_call | solution.py:604
  121.9 29.0 %store_results.1 = (bf16[256,256]{1,0:T(8,128)(2,1)}, f32[128,512]{1,0:T(8,128)}, f32[256,512]{1,0:T(8,128)}, f32[1,256]{1,0:T(1,128)}) custom-call(bf16[256,256]{1,0:T(8,128)(2,1)} %get-tuple-element.12.refs_0_, f32[128,512]{1,0:T(8,128)} %get-tuple-element.13.refs_1_, f32[256,512]{1,0:T(8,128)} %get-tuple-element.14.refs_2_, ...), custom_call_target="tpu_custom_call" | custom-call | tf_op jit(solution)/shard_map/store_results/pallas_call | solution.py:626

commit v5 on v4

--- a/solution.py
+++ b/solution.py
@@ -187,16 +187,19 @@
 
     lax.fori_loop(0, SIDE, turn, 0)
 
+    arrived(along_u)
+    mine = w_parts.at[pl.ds(1, FEATS - 1), :, v]
+    along_v = [send(mine, mine, v_dev(e)) for e in range(1, SIDE)]
+
     arrived(msg_two_copies)
-    back_two_at = group(3 * tiles)
-
-    def back_two(d, t):
-        return describe(back_two_at + (d - 1) * tiles + t, gsend_two.at[d - 1, tile(t)],
-                        grecv_two.at[d - 1, tile(t)], u_dev(-d))
+    back_two_at = group(3)
+
+    def back_two(d):
+        return describe(back_two_at + d - 1, gsend_two.at[d - 1], grecv_two.at[d - 1], u_dev(-d))
 
     def back_two_step(j, carry):
-        d, t = (j // tiles + 1) % SIDE, j % tiles
-        ids = lax.broadcasted_iota(I32, (PART, rows_three), 0) + t * PART
+        d = (j + 1) % SIDE
+        ids = lax.broadcasted_iota(I32, (rows_two, rows_three), 0)
         picks = jnp.concatenate(
             [(ids == asks[e, pl.ds(d, 1), rows_two:]).astype(BF) for e in range(SIDE)], axis=1
         )
@@ -204,33 +207,16 @@
 
         @pl.when(d > 0)
         def _():
-            gsend_two[d - 1, tile(t)] = value.astype(BF)
-            back_two(d, t).start()
+            gsend_two[d - 1] = value.astype(BF)
+            back_two(d).start()
 
         @pl.when(d == 0)
         def _():
-            gsum_two[tile(t)] = value
-
-        return carry
-
-    lax.fori_loop(0, SIDE * tiles, back_two_step, 0)
-    arrived(along_u)
-    mine = w_parts.at[pl.ds(1, FEATS - 1), :, v]
-    along_v = [send(mine, mine, v_dev(e)) for e in range(1, SIDE)]
-
-    for copy in small_loads:
-        copy.wait()
-    arrived([back_two(d, t) for d in range(1, SIDE) for t in range(tiles)])
-    gproj_two[:rows_three, :256] = cot[...].astype(BF)
-    gproj_two[rows_three:, :256] = jnp.zeros((rows_two - rows_three, 256), BF)
-
-    def ghid_step(t, carry):
-        total = add_up(gsum_two[tile(t, 128)], [grecv_two[d, tile(t, 128)] for d in range(3)])
-        gproj_two[tile(t, 128), 256:] = total.astype(BF)
-        ghid[tile(t, 128)] = dot(gproj_two[tile(t, 128)], w_two[...], ((1,), (1,)))
-        return carry
-
-    lax.fori_loop(0, rows_two // 128, ghid_step, 0)
+            gsum_two[...] = value
+
+        return carry
+
+    lax.fori_loop(0, SIDE, back_two_step, 0)
 
     arrived(along_v)
     w_one_load.wait()
@@ -270,33 +256,44 @@
             def _():
                 self_one[tile(c)] = dot(block, w_full[:, :256])
 
-        @pl.when(c > 0)
-        def _():
-            arrived([table_copy(c - 1, d) for d in others])
-
-            def sum_step(j, inner):
-                h, e = j // SIDE, (j + 1) % SIDE
-                ids = lax.broadcasted_iota(I32, (PART, PART), 1) + (c - 1) * PART
-                picks = jnp.concatenate(
-                    [(ids == asks_col[e, tile(h), d:d + 1]).astype(BF) for d in range(SIDE)],
-                    axis=1,
-                )
-                rows = jnp.concatenate([table[d, tile(c - 1)] for d in range(SIDE)], axis=0)
-                value = ysum[e, tile(h)] + dot(picks, rows)
-                ysum[e, tile(h)] = value
-
-                @pl.when((c == chunks) & (e > 0))
+        @pl.when(c > 1)
+        def _():
+            b = c - 2
+            arrived([table_copy(b, d) for d in others])
+
+            def sum_step(h, inner):
+                ids = lax.broadcasted_iota(I32, (PART, PART), 1) + b * PART
+                rows = jnp.concatenate([table[d, tile(b)] for d in range(SIDE)], axis=0)
+                for e in (2, 1, 3, 0):
+                    picks = jnp.concatenate(
+                        [(ids == asks_col[e, tile(h), d:d + 1]).astype(BF)
+                         for d in range(SIDE)], axis=1
+                    )
+                    ysum[e, tile(h)] += dot(picks, rows)
+
+                @pl.when(b == chunks - 1)
                 def _():
-                    ysend[e - 1, tile(h)] = value.astype(BF)
-                    y_copy(e, h).start()
+                    for e in others:
+                        ysend[e - 1, tile(h)] = ysum[e, tile(h)].astype(BF)
+                        y_copy(e, h).start()
 
                 return inner
 
-            lax.fori_loop(0, SIDE * tiles, sum_step, 0)
-
-        return carry
-
-    lax.fori_loop(0, chunks + 1, chunk_step, 0)
+            lax.fori_loop(0, tiles, sum_step, 0)
+
+        return carry
+
+    lax.fori_loop(0, chunks + 2, chunk_step, 0)
+
+    for copy in small_loads:
+        copy.wait()
+    arrived([back_two(d) for d in others])
+    gproj_two[:rows_three, :256] = cot[...].astype(BF)
+    gproj_two[rows_three:, :256] = jnp.zeros((rows_two - rows_three, 256), BF)
+
+    total = add_up(gsum_two[...], [grecv_two[d] for d in range(SIDE - 1)])
+    gproj_two[:, 256:] = total.astype(BF)
+    ghid[...] = dot(gproj_two[...], w_two[...], ((1,), (1,)))
 
     msg_at = group(3 * tiles)
 
@@ -308,7 +305,7 @@
         arrived([y_copy(e, h) for e in others])
 
         def rows_step(t, inner):
-            rows = pl.ds(pl.multiple_of(h * PART + t * 64, 64), 64)
+            rows = pl.ds(pl.multiple_of(h * PART + t * 128, 128), 128)
             total = add_up(ysum[0, rows], [yrecv[e, rows] for e in range(SIDE - 1)])
             linear = self_one[rows] + b_one[...] + total / FAN
             logistic = 1.0 / (1.0 + jnp.exp(-linear))
@@ -319,23 +316,19 @@
             bias[...] += jnp.sum(grad, axis=0, keepdims=True)
             return inner
 
-        lax.fori_loop(0, PART // 64, rows_step, 0)
+        lax.fori_loop(0, PART // 128, rows_step, 0)
         for e in others:
             msg_copy(h, e).start()
         return carry
 
     lax.fori_loop(0, tiles, act_step, 0)
 
-    def gw_two_step(k, carry):
-        value = dot(hidden[:, tile(k, 128)], gproj_two[...], ((0,), (0,))).astype(BF)
-        for r in range(2):
-            for q in range(4):
-                a, b = place(2 * k + r, q)
-                two_out[a, b, :64] = value[r * 64:r * 64 + 64, q * 128:q * 128 + 128]
-                two_out[a, b, 64:] = jnp.zeros((16, 128), BF)
-        return carry
-
-    lax.fori_loop(0, 2, gw_two_step, 0)
+    value = dot(hidden[...], gproj_two[...], ((0,), (0,))).astype(BF)
+    for r in range(4):
+        for q in range(4):
+            a, b = place(r, q)
+            two_out[a, b, :64] = value[r * 64:r * 64 + 64, q * 128:q * 128 + 128]
+            two_out[a, b, 64:] = jnp.zeros((16, 128), BF)
     for q in range(2):
         a, b = place(0, q)
         two_out[a, b, 64:] = jnp.broadcast_to(bias[:, q * 128:q * 128 + 128], (16, 128)).astype(BF)
@@ -343,28 +336,19 @@
         send(two_out.at[(u + d) % SIDE], two_in.at[d - 1], u_dev(d)) for d in others
     ]
 
-    def proj_two_step(t, carry):
-        proj = dot(hidden[tile(t, 128)], w_two[...])
-        table_two[0, tile(t, 128)] = proj[:, 256:].astype(BF)
-
-        @pl.when(t < rows_three // 128)
-        def _():
-            self_two[tile(t, 128)] = proj[:, :256]
-
-        return carry
-
-    lax.fori_loop(0, rows_two // 128, proj_two_step, 0)
+    proj = dot(hidden[...], w_two[...])
+    table_two[0] = proj[:, 256:].astype(BF)
+    self_two[...] = proj[:rows_three, :256]
     table_two_copies = [send(table_two.at[0], table_two.at[d], u_dev(d)) for d in others]
 
     two_v_at = group(3)
-    back_at = group(3 * chunks)
+    back_at = group(3)
 
     def two_v_copy(e):
         return describe(two_v_at + e - 1, two_mid.at[(v + e) % SIDE], two_v.at[e - 1], v_dev(e))
 
-    def back_copy(d, t):
-        return describe(back_at + (d - 1) * chunks + t, gsend.at[d - 1, tile(t)],
-                        grecv.at[d - 1, tile(t)], u_dev(-d))
+    def back_copy(d):
+        return describe(back_at + d - 1, gsend.at[d - 1], grecv.at[d - 1], u_dev(-d))
 
     def back_step(h, carry):
         @pl.when(h == tiles - 1)
@@ -380,23 +364,22 @@
         arrived([msg_copy(h, e) for e in others])
 
         def grad_step(j, inner):
-            d, t = (j // chunks + 1) % SIDE, j % chunks
-            ids = lax.broadcasted_iota(I32, (PART, PART), 0) + t * PART
+            d = (j + 1) % SIDE
+            ids = lax.broadcasted_iota(I32, (rows_one, PART), 0)
             picks = jnp.concatenate(
                 [(ids == asks[e, pl.ds(d, 1), tile(h)]).astype(BF) for e in range(SIDE)], axis=1
             )
             rows = jnp.concatenate([msg_one[e, tile(h)] for e in range(SIDE)], axis=0)
-            value = gsum[d, tile(t)] + dot(picks, rows)
-            gsum[d, tile(t)] = value
+            gsum[d] += dot(picks, rows)
 
             @pl.when((h == tiles - 1) & (d > 0))
             def _():
-                gsend[d - 1, tile(t)] = value.astype(BF)
-                back_copy(d, t).start()
+                gsend[d - 1] = gsum[d].astype(BF)
+                back_copy(d).start()
 
             return inner
 
-        lax.fori_loop(0, SIDE * chunks, grad_step, 0)
+        lax.fori_loop(0, SIDE, grad_step, 0)
         return carry
 
     lax.fori_loop(0, tiles, back_step, 0)
@@ -407,40 +390,38 @@
     ]
 
     arrived(table_two_copies)
-    y_two_at = group(6)
-
-    def y_two_copy(e, h):
-        return describe(y_two_at + h * 3 + e - 1, ysend_two.at[e - 1, tile(h, 128)],
-                        yrecv_two.at[e - 1, tile(h, 128)], v_dev(-e))
+    y_two_at = group(3)
+
+    def y_two_copy(e):
+        return describe(y_two_at + e - 1, ysend_two.at[e - 1], yrecv_two.at[e - 1], v_dev(-e))
 
     def y_two_step(j, carry):
-        e, h = (j // 2 + 1) % SIDE, j % 2
-        ids = lax.broadcasted_iota(I32, (128, rows_two), 1)
-        lower = pl.ds(pl.multiple_of(rows_two + h * 128, 128), 128)
+        e = (j + 1) % SIDE
+        ids = lax.broadcasted_iota(I32, (rows_three, rows_two), 1)
         picks = jnp.concatenate(
-            [(ids == asks_col[e, lower, d:d + 1]).astype(BF) for d in range(SIDE)], axis=1
+            [(ids == asks_col[e, rows_two:, d:d + 1]).astype(BF) for d in range(SIDE)], axis=1
         )
         value = dot(picks, jnp.concatenate([table_two[d] for d in range(SIDE)], axis=0))
 
         @pl.when(e > 0)
         def _():
-            ysend_two[e - 1, tile(h, 128)] = value.astype(BF)
-            y_two_copy(e, h).start()
+            ysend_two[e - 1] = value.astype(BF)
+            y_two_copy(e).start()
 
         @pl.when(e == 0)
         def _():
-            ysum_two[tile(h, 128)] = value
-
-        return carry
-
-    lax.fori_loop(0, 2 * SIDE, y_two_step, 0)
+            ysum_two[...] = value
+
+        return carry
+
+    lax.fori_loop(0, SIDE, y_two_step, 0)
 
     arrived(two_z_copies)
     two_all[u, v] = add_up(
         two_z[0].astype(F32), [two_z[i] for i in range(1, FEATS)]
     ).astype(BF)
     two_copies = [send(two_all.at[u, v], two_all.at[u, v], v_dev(e)) for e in others]
-    arrived([y_two_copy(e, h) for e in others for h in range(2)])
+    arrived([y_two_copy(e) for e in others])
 
     def out_step(t, carry):
         total = add_up(ysum_two[tile(t, 64)], [yrecv_two[e, tile(t, 64)] for e in range(3)])
@@ -451,45 +432,27 @@
     arrived(two_copies)
     two_copies = [send(two_all.at[u], two_all.at[u], u_dev(d)) for d in others]
 
-    arrived([back_copy(d, t) for d in others for t in range(chunks)])
-
-    def gtab_step(t, carry):
-        gtab[tile(t, 128)] = add_up(
-            gsum[0, tile(t, 128)], [grecv[d, tile(t, 128)] for d in range(SIDE - 1)]
-        ).astype(BF)
-        return carry
-
-    lax.fori_loop(0, rows_one // 128, gtab_step, 0)
-    pair_at = group(1)
-    pair = describe(pair_at, pair_out, pair_in, feat_dev(0, 1))
-
-    def outer_step(k, carry):
-        block = slab[2 * (k % 4) + 1 - k // 4]
-        wall[k, :, :256] = dot(block[:rows_two], glin[...], ((0,), (0,)))
-        wall[k, :, 256:] = dot(block, gtab[...], ((0,), (0,)))
-
-        @pl.when(k < 4)
-        def _():
-            pair_out[k] = wall[k].astype(BF)
-
-        @pl.when(k == 3)
-        def _():
-            pair.start()
-
-        return carry
-
-    lax.fori_loop(0, FEATS, outer_step, 0)
-    pair.wait_recv()
-
-    def piece_step(dz, carry):
-        value = (wall[4 + dz] + pair_in[dz].astype(F32)).astype(BF)
-        for r in range(4):
-            for q in range(4):
-                a, b = place(r, q)
-                w_out[a, b, tile(dz, 32)] = value[r * 32:r * 32 + 32, q * 128:q * 128 + 128]
-        return carry
-
-    lax.fori_loop(0, 4, piece_step, 0)
+    def outer(dc, grad):
+        block = jnp.concatenate([slab[2 * dz + dc] for dz in range(4)], axis=1)
+        return dot(block[:grad.shape[0]], grad[...], ((0,), (0,)))
+
+    pair_out[0] = outer(1, glin).astype(BF)
+    wall[0] = outer(0, glin)
+    pairs = [send(pair_out.at[0], pair_in.at[0], feat_dev(0, 1))]
+    arrived([back_copy(d) for d in others])
+    gtab[...] = add_up(gsum[0], [grecv[d] for d in range(SIDE - 1)]).astype(BF)
+    pair_out[1] = outer(1, gtab).astype(BF)
+    pairs.append(send(pair_out.at[1], pair_in.at[1], feat_dev(0, 1)))
+    wall[1] = outer(0, gtab)
+    arrived(pairs)
+    for k in range(2):
+        value = (wall[k] + pair_in[k].astype(F32)).astype(BF)
+        for dz in range(4):
+            for r in range(4):
+                for q in range(2):
+                    a, b = place(r, 2 * k + q)
+                    w_out[a, b, dz * 32:dz * 32 + 32] = value[
+                        dz * 128 + r * 32:dz * 128 + r * 32 + 32, q * 128:q * 128 + 128]
 
     sums = [send(w_out.at[(u + d) % SIDE], w_in.at[d - 1], u_dev(d)) for d in others]
     arrived(two_copies)
@@ -537,21 +500,18 @@
     lax.fori_loop(0, 4, lay_one, 0)
     for copy in groups:
         copy.wait_send()
-    pair.wait_send()
 
     def sent(c, carry):
         for i in range(1, FEATS):
             slab_copy(c, i).wait_send()
         for d in others:
             table_copy(c, d).wait_send()
-            back_copy(d, c).wait_send()
         return carry
 
     lax.fori_loop(0, chunks, sent, 0)
 
     def sent_tiles(t, carry):
         for d in others:
-            back_two(d, t).wait_send()
             y_copy(d, t).wait_send()
             msg_copy(t, d).wait_send()
         return carry
@@ -559,19 +519,9 @@
     lax.fori_loop(0, tiles, sent_tiles, 0)
     for e in others:
         two_v_copy(e).wait_send()
-        for h in range(2):
-            y_two_copy(e, h).wait_send()
-
-
-def store_kernel(*refs):
-    count = len(refs) // 2
-    copies = [
-        pltpu.make_async_copy(refs[i], refs[count + i], refs[-1].at[i]) for i in range(count)
-    ]
-    for copy in copies:
-        copy.start()
-    for copy in copies:
-        copy.wait()
+        y_two_copy(e).wait_send()
+        back_two(e).wait_send()
+        back_copy(e).wait_send()
 
 
 N_COPIES = 160
@@ -596,12 +546,12 @@
         ((3, r1, 256), BF), ((3, r1, 256), BF), ((1, 256), F32),
         ((4, 4, 80, 128), BF), ((3, 4, 80, 128), BF), ((4, 80, 128), BF), ((3, 80, 128), BF),
         ((FEATS, 80, 128), BF), ((4, 4, 80, 128), BF),
-        ((FEATS, 128, 512), F32), ((r1, 256), BF), ((4, 128, 512), BF), ((4, 128, 512), BF),
+        ((2, 512, 256), F32), ((r1, 256), BF), ((2, 512, 256), BF), ((2, 512, 256), BF),
         ((4, 4, 128, 128), BF), ((3, 4, 128, 128), BF),
         ((4, 128, 128), BF), ((3, 128, 128), BF), ((128, 128), BF), ((3, 32, 128), BF),
         ((4, 4, 32, 128), BF),
     ]
-    outs = pl.pallas_call(
+    layer_out, gw_one, gw_two, gb = pl.pallas_call(
         step_kernel,
         out_shape=[
             jax.ShapeDtypeStruct((r3, 256), BF), jax.ShapeDtypeStruct((128, 512), F32),
@@ -622,16 +572,6 @@
         name="sage_step",
     )(features, w_one, w_two, b_one[None], b_two[None], owner_one[0].T, slot_one[0].T,
       owner_two[0].T, slot_two[0].T, cotangent[0])
-    hbm = pl.BlockSpec(memory_space=pl.ANY)
-    layer_out, gw_one, gw_two, gb = pl.pallas_call(
-        store_kernel,
-        out_shape=[jax.ShapeDtypeStruct(o.shape, o.dtype) for o in outs],
-        in_specs=[hbm] * 4,
-        out_specs=[hbm] * 4,
-        scratch_shapes=[pltpu.SemaphoreType.DMA((4,))],
-        compiler_params=pltpu.CompilerParams(vmem_limit_bytes=60 * 2**20),
-        name="store_results",
-    )(*outs)
     return layer_out[None], gw_one, gw_two, gb[0]
 
 

time: 151 us -> 117 us (0.77)
  Pallas kernels: 150 us -> 110 us
  local copies, waits for them, and re-layouts: 0 us -> 6.34 us
    pallas_call x1 -> x0, Pallas kernels: 29 us -> none  [on_device(): pl.pallas_call(store_kernel, out_shape=[jax.ShapeDtypeStruct(o.shape, o.d...]
    pallas_call x1, Pallas kernels: 121 us -> 110 us  [on_device(): pl.pallas_call(step_kernel, out_shape=[jax.ShapeDtypeStruct((r3, 256), BF...]
    unnamed x0 -> x4, local copies, waits for them, and re-layouts: none -> 6.34 us
where the time goes in v5:
time: 117 us
  Pallas kernels  110 us (94%)
  local copies, waits for them, and re-layouts  6.34 us (5%)
    pallas_call x1, Pallas kernels, on_device(): pl.pallas_call(step_kernel, out_shape=[jax.ShapeDtypeStruct((r3, 256), BF...  110 us
    unnamed x4, local copies, waits for them, and re-layouts  6.34 us

profile of v5, /device:TPU:0, one launch (start us, length us, event | category | flops | bytes accessed | tf_op | source)
XLA Modules:
  0.0 116.6 jit_solution(16202393640713597124)
XLA Ops:
  0.6 109.6 %sage_step.1 = (bf16[256,256]{1,0:T(8,128)(2,1)}, f32[128,512]{1,0:T(8,128)}, f32[256,512]{1,0:T(8,128)}, f32[1,256]{1,0:T(1,128)}) custom-call(bf16[8,1024,128]{2,1,0:T(8,128)(2,1)} %feat_ref.1, bf16[128,512]{1,0:T(8,128)(2,1)} %w_one_ref.1, bf16[256,512]{1,0:T(8,128)(2,1)} %w_two_ref.1, f32[1,256]{1,0:T(1,128)} %bitcast.24, f32[1,256]{1,0:T(1,128)} %bitcast.25, ...), custom_call_target="tpu_custom_call" | custom-call | flops 14000000000 | bytes 8388608 | tf_op jit(solution)/shard_map/sage_step/pallas_call | solution.py:554
  110.3 1.6 %copy.18 = bf16[1,256,256]{2,1,0:T(8,128)(2,1)} copy(bf16[1,256,256]{2,1,0:T(8,128)(2,1)} %bitcast.17) | data formatting | bytes 262144
  111.8 1.7 %copy.19 = f32[128,512]{1,0:T(8,128)} copy(f32[128,512]{1,0:T(8,128)} %get-tuple-element.17) | data formatting | bytes 524288
  113.5 1.9 %copy.20 = f32[256,512]{1,0:T(8,128)} copy(f32[256,512]{1,0:T(8,128)} %get-tuple-element.18) | data formatting | bytes 1048576
  115.4 1.2 %copy.21 = f32[256]{0:T(256)} copy(f32[256]{0:T(256)} %bitcast.18) | data formatting | bytes 2048

commit v6 on v5

--- a/solution.py
+++ b/solution.py
@@ -120,6 +120,27 @@
     own_load = load(feat_ref.at[f], slab.at[0])
     small_loads = [load(w_two_ref, w_two), load(b_one_ref, b_one), load(b_two_ref, b_two)]
 
+    pl.semaphore_wait(barrier, len(partners))
+
+    low, high = n % SIDE, n // SIDE
+    w_piece = w_one_ref.at[pl.ds(pl.multiple_of(high * 32, 32), 32),
+                           pl.ds(pl.multiple_of(low * 128, 128), 128)]
+    w_copies = [send(w_piece, w_parts.at[dz - 1, u, v], feat_dev(dz, 0)) for dz in others]
+    slab_at = group(7 * chunks)
+
+    def slab_copy(c, i):
+        dev = feat_dev(*slots[i])
+        return describe(slab_at + c * 7 + i - 1, feat_ref.at[dev[0], tile(c)],
+                        slab.at[i, tile(c)], dev)
+
+    def send_chunk(c, carry):
+        for i in (4, 5, 2, 3, 6, 7, 1):
+            slab_copy(c, i).start()
+        return carry
+
+    send_chunk(0, 0)
+    w_pairs = [send(w_one_ref, w_full.at[pl.ds(128, 128)], feat_dev(0, 1))]
+
     for copy in index_loads:
         copy.wait()
 
@@ -138,58 +159,32 @@
     cot_load.wait()
     msg_two[0] = (cot[...] / FAN).astype(BF)
 
+    ask_copies = [send(asks_out.at[e], asks.at[e], v_dev(e)) for e in range(1, SIDE)]
+    msg_two_copies = [send(msg_two.at[0], msg_two.at[e], v_dev(e)) for e in range(1, SIDE)]
+    send_chunk(1, 0)
+
+    arrived(w_copies)
+    mine = w_parts.at[:, u, v]
+    along_u = [send(mine, mine, u_dev(d)) for d in range(1, SIDE)]
+    lax.fori_loop(2, chunks, send_chunk, 0)
+    asks[0] = asks_out[0]
+    arrived(ask_copies)
+
+    def turn(e, carry):
+        asks_col[e] = jnp.transpose(asks[e].astype(F32)).astype(I32)
+        return carry
+
+    lax.fori_loop(0, SIDE, turn, 0)
+    arrived(along_u)
+    mine = w_parts.at[:, :, v]
+    along_v = [send(mine, mine, v_dev(e)) for e in range(1, SIDE)]
+
     def clear(j, carry):
         ysum[j] = jnp.zeros((rows_two, 256), F32)
-        gsum[j] = jnp.zeros((rows_one, 256), F32)
         return carry
 
     lax.fori_loop(0, SIDE, clear, 0)
     bias[...] = jnp.zeros((1, 256), F32)
-
-    pl.semaphore_wait(barrier, len(partners))
-
-    low, high = n % SIDE, n // SIDE
-    w_copies = []
-    for i, (dz, dc) in enumerate(slots):
-        if i:
-            their_u, their_v = line_place((core + dc) % 2, n)
-            w_copies.append(send(
-                w_one_ref.at[pl.ds(pl.multiple_of(high * 32, 32), 32),
-                             pl.ds(pl.multiple_of(low * 128, 128), 128)],
-                w_parts.at[i, their_u, their_v], feat_dev(dz, dc),
-            ))
-    slab_at = group(7 * chunks)
-
-    def slab_copy(c, i):
-        dev = feat_dev(*slots[i])
-        return describe(slab_at + c * 7 + i - 1, feat_ref.at[dev[0], tile(c)],
-                        slab.at[i, tile(c)], dev)
-
-    def send_chunk(c, carry):
-        for i in (4, 5, 2, 3, 6, 7, 1):
-            slab_copy(c, i).start()
-        return carry
-
-    send_chunk(0, 0)
-    ask_copies = [send(asks_out.at[e], asks.at[e], v_dev(e)) for e in range(1, SIDE)]
-    msg_two_copies = [send(msg_two.at[0], msg_two.at[e], v_dev(e)) for e in range(1, SIDE)]
-    lax.fori_loop(1, chunks, send_chunk, 0)
-
-    arrived(w_copies)
-    mine = w_parts.at[pl.ds(1, FEATS - 1), u, v]
-    along_u = [send(mine, mine, u_dev(d)) for d in range(1, SIDE)]
-    asks[0] = asks_out[0]
-    arrived(ask_copies)
-
-    def turn(e, carry):
-        asks_col[e] = jnp.transpose(asks[e].astype(F32)).astype(I32)
-        return carry
-
-    lax.fori_loop(0, SIDE, turn, 0)
-
-    arrived(along_u)
-    mine = w_parts.at[pl.ds(1, FEATS - 1), :, v]
-    along_v = [send(mine, mine, v_dev(e)) for e in range(1, SIDE)]
 
     arrived(msg_two_copies)
     back_two_at = group(3)
@@ -221,15 +216,16 @@
     arrived(along_v)
     w_one_load.wait()
 
-    def lay_w(i, carry):
+    for dz in range(1, SIDE):
         for r in range(4):
             for q in range(4):
                 a, b = place(r, q)
-                w_full[pl.ds(pl.multiple_of(i * 128 + r * 32, 32), 32),
-                       q * 128:q * 128 + 128] = w_parts[i, a, b]
-        return carry
-
-    lax.fori_loop(1, FEATS, lay_w, 0)
+                w_full[dz * 256 + r * 32:dz * 256 + r * 32 + 32, q * 128:q * 128 + 128] = (
+                    w_parts[dz - 1, a, b]
+                )
+        w_pairs.append(send(w_full.at[pl.ds(dz * 256, 128)],
+                            w_full.at[pl.ds(dz * 256 + 128, 128)], feat_dev(0, 1)))
+    arrived(w_pairs)
     own_load.wait()
 
     table_at = group(3 * chunks)
@@ -350,39 +346,42 @@
     def back_copy(d):
         return describe(back_at + d - 1, gsend.at[d - 1], grecv.at[d - 1], u_dev(-d))
 
-    def back_step(h, carry):
-        @pl.when(h == tiles - 1)
-        def _():
-            arrived(two_u_copies)
-            for b in range(SIDE):
-                two_mid[b] = add_up(
-                    two_out[u, b].astype(F32), [two_in[d, b] for d in range(SIDE - 1)]
-                ).astype(BF)
-            for e in others:
-                two_v_copy(e).start()
-
-        arrived([msg_copy(h, e) for e in others])
-
-        def grad_step(j, inner):
-            d = (j + 1) % SIDE
-            ids = lax.broadcasted_iota(I32, (rows_one, PART), 0)
-            picks = jnp.concatenate(
-                [(ids == asks[e, pl.ds(d, 1), tile(h)]).astype(BF) for e in range(SIDE)], axis=1
-            )
-            rows = jnp.concatenate([msg_one[e, tile(h)] for e in range(SIDE)], axis=0)
-            gsum[d] += dot(picks, rows)
-
-            @pl.when((h == tiles - 1) & (d > 0))
-            def _():
-                gsend[d - 1] = gsum[d].astype(BF)
-                back_copy(d).start()
-
-            return inner
-
-        lax.fori_loop(0, SIDE, grad_step, 0)
-        return carry
-
-    lax.fori_loop(0, tiles, back_step, 0)
+    def line_grads(e, d):
+        ids = lax.broadcasted_iota(I32, (rows_one, rows_two), 0)
+        return dot((ids == asks[e, pl.ds(d, 1), :rows_two]).astype(BF), msg_one[e])
+
+    def own_step(d, carry):
+        gsum[d] = line_grads(0, d)
+        return carry
+
+    lax.fori_loop(0, SIDE, own_step, 0)
+    arrived(two_u_copies)
+    for b in range(SIDE):
+        two_mid[b] = add_up(
+            two_out[u, b].astype(F32), [two_in[d, b] for d in range(SIDE - 1)]
+        ).astype(BF)
+    for e in others:
+        two_v_copy(e).start()
+    arrived([msg_copy(h, e) for h in range(tiles) for e in others])
+
+    def back_step(j, carry):
+        d = (j + 1) % SIDE
+        value = gsum[d]
+        for e in range(1, SIDE):
+            value += line_grads(e, d)
+
+        @pl.when(d > 0)
+        def _():
+            gsend[d - 1] = value.astype(BF)
+            back_copy(d).start()
+
+        @pl.when(d == 0)
+        def _():
+            gsum[0] = value
+
+        return carry
+
+    lax.fori_loop(0, SIDE, back_step, 0)
     arrived([two_v_copy(e) for e in others])
     two_z[0] = add_up(two_mid[v].astype(F32), [two_v[e] for e in range(SIDE - 1)]).astype(BF)
     two_z_copies = [
@@ -533,7 +532,7 @@
     r1, r2, r3 = features.shape[1], owner_one.shape[1], owner_two.shape[1]
     vm = pl.BlockSpec(memory_space=pltpu.VMEM)
     scratch = [
-        ((FEATS, r1, 128), BF), ((FEATS, 4, 4, 32, 128), BF), ((1024, 512), BF),
+        ((FEATS, r1, 128), BF), ((3, 4, 4, 32, 128), BF), ((1024, 512), BF),
         ((256, 512), BF), ((1, 256), F32), ((1, 256), F32),
         ((FAN, r2), I32), ((FAN, r2), I32), ((FAN, r3), I32), ((FAN, r3), I32),
         ((r3, 256), F32), ((SIDE, 8, r2 + r3), I32),

time: 117 us -> 113 us (0.966)
  Pallas kernels: 110 us -> 105 us
    pallas_call x1, Pallas kernels: 110 us -> 105 us  [on_device(): pl.pallas_call(step_kernel, out_shape=[jax.ShapeDtypeStruct((r3, 256), BF...]
where the time goes in v6:
time: 113 us; the launch traced here: 112 us
  Pallas kernels  105 us (93%)
  local copies, waits for them, and re-layouts  6.34 us (6%)
    pallas_call x1, Pallas kernels, on_device(): pl.pallas_call(step_kernel, out_shape=[jax.ShapeDtypeStruct((r3, 256), BF...  105 us
    unnamed x4, local copies, waits for them, and re-layouts  6.34 us

profile of v6, /device:TPU:0, one launch (start us, length us, event | category | flops | bytes accessed | tf_op | source)
XLA Modules:
  0.0 112.4 jit_solution(6290924442486816430)
XLA Ops:
  0.6 105.4 %sage_step.1 = (bf16[256,256]{1,0:T(8,128)(2,1)}, f32[128,512]{1,0:T(8,128)}, f32[256,512]{1,0:T(8,128)}, f32[1,256]{1,0:T(1,128)}) custom-call(bf16[8,1024,128]{2,1,0:T(8,128)(2,1)} %feat_ref.1, bf16[128,512]{1,0:T(8,128)(2,1)} %w_one_ref.1, bf16[256,512]{1,0:T(8,128)(2,1)} %w_two_ref.1, f32[1,256]{1,0:T(1,128)} %bitcast.24, f32[1,256]{1,0:T(1,128)} %bitcast.25, ...), custom_call_target="tpu_custom_call" | custom-call | flops 14000000000 | bytes 8388608 | tf_op jit(solution)/shard_map/sage_step/pallas_call | solution.py:553
  106.0 1.6 %copy.18 = bf16[1,256,256]{2,1,0:T(8,128)(2,1)} copy(bf16[1,256,256]{2,1,0:T(8,128)(2,1)} %bitcast.17) | data formatting | bytes 262144
  107.6 1.7 %copy.19 = f32[128,512]{1,0:T(8,128)} copy(f32[128,512]{1,0:T(8,128)} %get-tuple-element.17) | data formatting | bytes 524288
  109.3 1.9 %copy.20 = f32[256,512]{1,0:T(8,128)} copy(f32[256,512]{1,0:T(8,128)} %get-tuple-element.18) | data formatting | bytes 1048576
  111.1 1.2 %copy.21 = f32[256]{0:T(256)} copy(f32[256]{0:T(256)} %bitcast.18) | data formatting | bytes 2048

commit v7 on v6

--- a/solution.py
+++ b/solution.py
@@ -355,6 +355,26 @@
         return carry
 
     lax.fori_loop(0, SIDE, own_step, 0)
+    arrived([msg_copy(h, e) for h in range(tiles) for e in others])
+
+    def back_step(j, carry):
+        d = (j + 1) % SIDE
+        value = gsum[d]
+        for e in range(1, SIDE):
+            value += line_grads(e, d)
+
+        @pl.when(d > 0)
+        def _():
+            gsend[d - 1] = value.astype(BF)
+            back_copy(d).start()
+
+        @pl.when(d == 0)
+        def _():
+            gsum[0] = value
+
+        return carry
+
+    lax.fori_loop(0, SIDE, back_step, 0)
     arrived(two_u_copies)
     for b in range(SIDE):
         two_mid[b] = add_up(
@@ -362,31 +382,6 @@
         ).astype(BF)
     for e in others:
         two_v_copy(e).start()
-    arrived([msg_copy(h, e) for h in range(tiles) for e in others])
-
-    def back_step(j, carry):
-        d = (j + 1) % SIDE
-        value = gsum[d]
-        for e in range(1, SIDE):
-            value += line_grads(e, d)
-
-        @pl.when(d > 0)
-        def _():
-            gsend[d - 1] = value.astype(BF)
-            back_copy(d).start()
-
-        @pl.when(d == 0)
-        def _():
-            gsum[0] = value
-
-        return carry
-
-    lax.fori_loop(0, SIDE, back_step, 0)
-    arrived([two_v_copy(e) for e in others])
-    two_z[0] = add_up(two_mid[v].astype(F32), [two_v[e] for e in range(SIDE - 1)]).astype(BF)
-    two_z_copies = [
-        send(two_z.at[0], two_z.at[i], feat_dev(*slots[i])) for i in range(1, FEATS)
-    ]
 
     arrived(table_two_copies)
     y_two_at = group(3)
@@ -415,34 +410,40 @@
 
     lax.fori_loop(0, SIDE, y_two_step, 0)
 
+    arrived([two_v_copy(e) for e in others])
+    two_z[0] = add_up(two_mid[v].astype(F32), [two_v[e] for e in range(SIDE - 1)]).astype(BF)
+    two_z_copies = [
+        send(two_z.at[0], two_z.at[i], feat_dev(*slots[i])) for i in range(1, FEATS)
+    ]
+
+    def outer(dc, grad):
+        block = jnp.concatenate([slab[2 * dz + dc] for dz in range(4)], axis=1)
+        return dot(block[:grad.shape[0]], grad[...], ((0,), (0,)))
+
+    pair_out[0] = outer(1, glin).astype(BF)
+    wall[0] = outer(0, glin)
+    pairs = [send(pair_out.at[0], pair_in.at[0], feat_dev(0, 1))]
+    arrived([y_two_copy(e) for e in others])
+
+    def out_step(t, carry):
+        total = add_up(ysum_two[tile(t, 64)], [yrecv_two[e, tile(t, 64)] for e in range(3)])
+        out_ref[tile(t, 64)] = (self_two[tile(t, 64)] + b_two[...] + total / FAN).astype(BF)
+        return carry
+
+    lax.fori_loop(0, rows_three // 64, out_step, 0)
+
     arrived(two_z_copies)
     two_all[u, v] = add_up(
         two_z[0].astype(F32), [two_z[i] for i in range(1, FEATS)]
     ).astype(BF)
     two_copies = [send(two_all.at[u, v], two_all.at[u, v], v_dev(e)) for e in others]
-    arrived([y_two_copy(e) for e in others])
-
-    def out_step(t, carry):
-        total = add_up(ysum_two[tile(t, 64)], [yrecv_two[e, tile(t, 64)] for e in range(3)])
-        out_ref[tile(t, 64)] = (self_two[tile(t, 64)] + b_two[...] + total / FAN).astype(BF)
-        return carry
-
-    lax.fori_loop(0, rows_three // 64, out_step, 0)
-    arrived(two_copies)
-    two_copies = [send(two_all.at[u], two_all.at[u], u_dev(d)) for d in others]
-
-    def outer(dc, grad):
-        block = jnp.concatenate([slab[2 * dz + dc] for dz in range(4)], axis=1)
-        return dot(block[:grad.shape[0]], grad[...], ((0,), (0,)))
-
-    pair_out[0] = outer(1, glin).astype(BF)
-    wall[0] = outer(0, glin)
-    pairs = [send(pair_out.at[0], pair_in.at[0], feat_dev(0, 1))]
     arrived([back_copy(d) for d in others])
     gtab[...] = add_up(gsum[0], [grecv[d] for d in range(SIDE - 1)]).astype(BF)
     pair_out[1] = outer(1, gtab).astype(BF)
     pairs.append(send(pair_out.at[1], pair_in.at[1], feat_dev(0, 1)))
     wall[1] = outer(0, gtab)
+    arrived(two_copies)
+    two_copies = [send(two_all.at[u], two_all.at[u], u_dev(d)) for d in others]
     arrived(pairs)
     for k in range(2):
         value = (wall[k] + pair_in[k].astype(F32)).astype(BF)
@@ -521,6 +522,19 @@
         y_two_copy(e).wait_send()
         back_two(e).wait_send()
         back_copy(e).wait_send()
+
+
+def store_kernel(*refs):
+    src, dst, held, sem = refs[:4], refs[4:8], refs[8:12], refs[12]
+    reads = [pltpu.make_async_copy(src[i], held[i], sem.at[i]) for i in range(4)]
+    writes = [pltpu.make_async_copy(held[i], dst[i], sem.at[4 + i]) for i in range(4)]
+    for copy in reads:
+        copy.start()
+    for read, write in zip(reads, writes):
+        read.wait()
+        write.start()
+    for copy in writes:
+        copy.wait()
 
 
 N_COPIES = 160
@@ -550,7 +564,7 @@
         ((4, 128, 128), BF), ((3, 128, 128), BF), ((128, 128), BF), ((3, 32, 128), BF),
         ((4, 4, 32, 128), BF),
     ]
-    layer_out, gw_one, gw_two, gb = pl.pallas_call(
+    outs = pl.pallas_call(
         step_kernel,
         out_shape=[
             jax.ShapeDtypeStruct((r3, 256), BF), jax.ShapeDtypeStruct((128, 512), F32),
@@ -571,6 +585,17 @@
         name="sage_step",
     )(features, w_one, w_two, b_one[None], b_two[None], owner_one[0].T, slot_one[0].T,
       owner_two[0].T, slot_two[0].T, cotangent[0])
+    anywhere = pl.BlockSpec(memory_space=pl.ANY)
+    layer_out, gw_one, gw_two, gb = pl.pallas_call(
+        store_kernel,
+        out_shape=[jax.ShapeDtypeStruct(o.shape, o.dtype) for o in outs],
+        in_specs=[anywhere] * 4,
+        out_specs=[anywhere] * 4,
+        scratch_shapes=[pltpu.VMEM(o.shape, o.dtype) for o in outs]
+        + [pltpu.SemaphoreType.DMA((8,))],
+        compiler_params=pltpu.CompilerParams(vmem_limit_bytes=56 * 2**20),
+        name="store_results",
+    )(*outs)
     return layer_out[None], gw_one, gw_two, gb[0]
 
 

time: 113 us -> 109 us (0.965)
  local copies, waits for them, and re-layouts: 6.34 us -> 0 us
  Pallas kernels: 105 us -> 108 us
    unnamed x4 -> x0, local copies, waits for them, and re-layouts: 6.34 us -> none
    pallas_call x0 -> x1, Pallas kernels: none -> 2.06 us  [on_device(): pl.pallas_call(store_kernel, out_shape=[jax.ShapeDtypeStruct(o.shape, o.d...]
where the time goes in v7:
time: 109 us
  Pallas kernels  108 us (99%)
    pallas_call x1, Pallas kernels, on_device(): pl.pallas_call(step_kernel, out_shape=[jax.ShapeDtypeStruct((r3, 256), BF...  106 us

profile of v7, /device:TPU:0, one launch (start us, length us, event | category | flops | bytes accessed | tf_op | source)
XLA Modules:
  0.0 108.9 jit_solution(11872879340656610288)
XLA Ops:
  0.6 106.2 %sage_step.1 = (bf16[256,256]{1,0:T(8,128)(2,1)}, f32[128,512]{1,0:T(8,128)}, f32[256,512]{1,0:T(8,128)}, f32[1,256]{1,0:T(1,128)}) custom-call(bf16[8,1024,128]{2,1,0:T(8,128)(2,1)} %feat_ref.1, bf16[128,512]{1,0:T(8,128)(2,1)} %w_one_ref.1, bf16[256,512]{1,0:T(8,128)(2,1)} %w_two_ref.1, f32[1,256]{1,0:T(1,128)} %bitcast.23, f32[1,256]{1,0:T(1,128)} %bitcast.24, ...), custom_call_target="tpu_custom_call" | custom-call | flops 14000000000 | bytes 8388608 | tf_op jit(solution)/shard_map/sage_step/pallas_call | solution.py:567
  106.9 2.1 %store_results.1 = (bf16[256,256]{1,0:T(8,128)(2,1)}, f32[128,512]{1,0:T(8,128)}, f32[256,512]{1,0:T(8,128)}, f32[1,256]{1,0:T(1,128)}) custom-call(bf16[256,256]{1,0:T(8,128)(2,1)} %get-tuple-element.12.refs_0_, f32[128,512]{1,0:T(8,128)} %get-tuple-element.13.refs_1_, f32[256,512]{1,0:T(8,128)} %get-tuple-element.14.refs_2_, ...), custom_call_target="tpu_custom_call" | custom-call | tf_op jit(solution)/shard_map/store_results/pallas_call | solution.py:589

commit v8 on v7

--- a/solution.py
+++ b/solution.py
@@ -335,7 +335,6 @@
     proj = dot(hidden[...], w_two[...])
     table_two[0] = proj[:, 256:].astype(BF)
     self_two[...] = proj[:rows_three, :256]
-    table_two_copies = [send(table_two.at[0], table_two.at[d], u_dev(d)) for d in others]
 
     two_v_at = group(3)
     back_at = group(3)
@@ -383,61 +382,25 @@
     for e in others:
         two_v_copy(e).start()
 
-    arrived(table_two_copies)
-    y_two_at = group(3)
-
-    def y_two_copy(e):
-        return describe(y_two_at + e - 1, ysend_two.at[e - 1], yrecv_two.at[e - 1], v_dev(-e))
-
-    def y_two_step(j, carry):
-        e = (j + 1) % SIDE
-        ids = lax.broadcasted_iota(I32, (rows_three, rows_two), 1)
-        picks = jnp.concatenate(
-            [(ids == asks_col[e, rows_two:, d:d + 1]).astype(BF) for d in range(SIDE)], axis=1
-        )
-        value = dot(picks, jnp.concatenate([table_two[d] for d in range(SIDE)], axis=0))
-
-        @pl.when(e > 0)
-        def _():
-            ysend_two[e - 1] = value.astype(BF)
-            y_two_copy(e).start()
-
-        @pl.when(e == 0)
-        def _():
-            ysum_two[...] = value
-
-        return carry
-
-    lax.fori_loop(0, SIDE, y_two_step, 0)
-
+    def outer(dc, grad):
+        block = jnp.concatenate([slab[2 * dz + dc] for dz in range(4)], axis=1)
+        return dot(block[:grad.shape[0]], grad[...], ((0,), (0,)))
+
+    pair_out[0] = outer(1, glin).astype(BF)
+    wall[0] = outer(0, glin)
+    pairs = [send(pair_out.at[0], pair_in.at[0], feat_dev(0, 1))]
     arrived([two_v_copy(e) for e in others])
     two_z[0] = add_up(two_mid[v].astype(F32), [two_v[e] for e in range(SIDE - 1)]).astype(BF)
     two_z_copies = [
         send(two_z.at[0], two_z.at[i], feat_dev(*slots[i])) for i in range(1, FEATS)
     ]
-
-    def outer(dc, grad):
-        block = jnp.concatenate([slab[2 * dz + dc] for dz in range(4)], axis=1)
-        return dot(block[:grad.shape[0]], grad[...], ((0,), (0,)))
-
-    pair_out[0] = outer(1, glin).astype(BF)
-    wall[0] = outer(0, glin)
-    pairs = [send(pair_out.at[0], pair_in.at[0], feat_dev(0, 1))]
-    arrived([y_two_copy(e) for e in others])
-
-    def out_step(t, carry):
-        total = add_up(ysum_two[tile(t, 64)], [yrecv_two[e, tile(t, 64)] for e in range(3)])
-        out_ref[tile(t, 64)] = (self_two[tile(t, 64)] + b_two[...] + total / FAN).astype(BF)
-        return carry
-
-    lax.fori_loop(0, rows_three // 64, out_step, 0)
-
     arrived(two_z_copies)
     two_all[u, v] = add_up(
         two_z[0].astype(F32), [two_z[i] for i in range(1, FEATS)]
     ).astype(BF)
     two_copies = [send(two_all.at[u, v], two_all.at[u, v], v_dev(e)) for e in others]
     arrived([back_copy(d) for d in others])
+    table_two_copies = [send(table_two.at[0], table_two.at[d], u_dev(d)) for d in others]
     gtab[...] = add_up(gsum[0], [grecv[d] for d in range(SIDE - 1)]).astype(BF)
     pair_out[1] = outer(1, gtab).astype(BF)
     pairs.append(send(pair_out.at[1], pair_in.at[1], feat_dev(0, 1)))
@@ -455,6 +418,34 @@
                         dz * 128 + r * 32:dz * 128 + r * 32 + 32, q * 128:q * 128 + 128]
 
     sums = [send(w_out.at[(u + d) % SIDE], w_in.at[d - 1], u_dev(d)) for d in others]
+
+    arrived(table_two_copies)
+    y_two_at = group(3)
+
+    def y_two_copy(e):
+        return describe(y_two_at + e - 1, ysend_two.at[e - 1], yrecv_two.at[e - 1], v_dev(-e))
+
+    def y_two_step(j, carry):
+        e = (j + 1) % SIDE
+        ids = lax.broadcasted_iota(I32, (rows_three, rows_two), 1)
+        picks = jnp.concatenate(
+            [(ids == asks_col[e, rows_two:, d:d + 1]).astype(BF) for d in range(SIDE)], axis=1
+        )
+        value = dot(picks, jnp.concatenate([table_two[d] for d in range(SIDE)], axis=0))
+
+        @pl.when(e > 0)
+        def _():
+            ysend_two[e - 1] = value.astype(BF)
+            y_two_copy(e).start()
+
+        @pl.when(e == 0)
+        def _():
+            ysum_two[...] = value
+
+        return carry
+
+    lax.fori_loop(0, SIDE, y_two_step, 0)
+
     arrived(two_copies)
 
     def lay_two(r, carry):
@@ -482,6 +473,15 @@
     sums = [
         send(z_out.at[pl.ds(dz * 32, 32)], z_in.at[dz - 1], feat_dev(-dz, 0)) for dz in others
     ]
+    arrived([y_two_copy(e) for e in others])
+
+    def out_step(t, carry):
+        total = add_up(ysum_two[tile(t, 64)], [yrecv_two[e, tile(t, 64)] for e in range(3)])
+        out_ref[tile(t, 64)] = (self_two[tile(t, 64)] + b_two[...] + total / FAN).astype(BF)
+        return carry
+
+    lax.fori_loop(0, rows_three // 64, out_step, 0)
+
     arrived(sums)
     piece_all[u, v] = add_up(
         z_out[:32].astype(F32), [z_in[dz] for dz in range(3)]

time: 109 us -> 110 us (level)
  Pallas kernels: 108 us -> 110 us
    pallas_call x1, Pallas kernels: 106 us -> 107 us  [on_device(): pl.pallas_call(step_kernel, out_shape=[jax.ShapeDtypeStruct((r3, 256), BF...]
where the time goes in v8:
time: 110 us
  Pallas kernels  110 us (100%)
    pallas_call x1, Pallas kernels, on_device(): pl.pallas_call(step_kernel, out_shape=[jax.ShapeDtypeStruct((r3, 256), BF...  107 us

profile of v8, /device:TPU:0, one launch (start us, length us, event | category | flops | bytes accessed | tf_op | source)
XLA Modules:
  0.0 110.2 jit_solution(18214827530435114455)
XLA Ops:
  0.6 107.4 %sage_step.1 = (bf16[256,256]{1,0:T(8,128)(2,1)}, f32[128,512]{1,0:T(8,128)}, f32[256,512]{1,0:T(8,128)}, f32[1,256]{1,0:T(1,128)}) custom-call(bf16[8,1024,128]{2,1,0:T(8,128)(2,1)} %feat_ref.1, bf16[128,512]{1,0:T(8,128)(2,1)} %w_one_ref.1, bf16[256,512]{1,0:T(8,128)(2,1)} %w_two_ref.1, f32[1,256]{1,0:T(1,128)} %bitcast.23, f32[1,256]{1,0:T(1,128)} %bitcast.24, ...), custom_call_target="tpu_custom_call" | custom-call | flops 14000000000 | bytes 8388608 | tf_op jit(solution)/shard_map/sage_step/pallas_call | solution.py:567
  108.1 2.1 %store_results.1 = (bf16[256,256]{1,0:T(8,128)(2,1)}, f32[128,512]{1,0:T(8,128)}, f32[256,512]{1,0:T(8,128)}, f32[1,256]{1,0:T(1,128)}) custom-call(bf16[256,256]{1,0:T(8,128)(2,1)} %get-tuple-element.12.refs_0_, f32[128,512]{1,0:T(8,128)} %get-tuple-element.13.refs_1_, f32[256,512]{1,0:T(8,128)} %get-tuple-element.14.refs_2_, ...), custom_call_target="tpu_custom_call" | custom-call | tf_op jit(solution)/shard_map/store_results/pallas_call | solution.py:589

commit v9 on v8

--- a/solution.py
+++ b/solution.py
@@ -399,8 +399,10 @@
         two_z[0].astype(F32), [two_z[i] for i in range(1, FEATS)]
     ).astype(BF)
     two_copies = [send(two_all.at[u, v], two_all.at[u, v], v_dev(e)) for e in others]
+    for d in others:
+        back_copy(d).wait_send()
+    table_two_copies = [send(table_two.at[0], table_two.at[d], u_dev(d)) for d in others]
     arrived([back_copy(d) for d in others])
-    table_two_copies = [send(table_two.at[0], table_two.at[d], u_dev(d)) for d in others]
     gtab[...] = add_up(gsum[0], [grecv[d] for d in range(SIDE - 1)]).astype(BF)
     pair_out[1] = outer(1, gtab).astype(BF)
     pairs.append(send(pair_out.at[1], pair_in.at[1], feat_dev(0, 1)))
@@ -419,6 +421,29 @@
 
     sums = [send(w_out.at[(u + d) % SIDE], w_in.at[d - 1], u_dev(d)) for d in others]
 
+    arrived(two_copies)
+
+    def lay_two(r, carry):
+        for q in range(4):
+            a, b = place(r, q)
+            gw_two_ref[tile(r, 64), q * 128:q * 128 + 128] = two_all[a, b, :64].astype(F32)
+        return carry
+
+    lax.fori_loop(0, 4, lay_two, 0)
+    for q in range(2):
+        a, b = place(0, q)
+        gb_ref[:, q * 128:q * 128 + 128] = two_all[a, b, 64:].astype(F32)[:1]
+    arrived(sums)
+
+    def mid_step(b, carry):
+        w_mid[b] = add_up(
+            w_out[u, b].astype(F32), [w_in[d, b] for d in range(SIDE - 1)]
+        ).astype(BF)
+        return carry
+
+    lax.fori_loop(0, SIDE, mid_step, 0)
+    sums = [send(w_mid.at[(v + e) % SIDE], v_in.at[e - 1], v_dev(e)) for e in others]
+
     arrived(table_two_copies)
     y_two_at = group(3)
 
@@ -446,42 +471,11 @@
 
     lax.fori_loop(0, SIDE, y_two_step, 0)
 
-    arrived(two_copies)
-
-    def lay_two(r, carry):
-        for q in range(4):
-            a, b = place(r, q)
-            gw_two_ref[tile(r, 64), q * 128:q * 128 + 128] = two_all[a, b, :64].astype(F32)
-        return carry
-
-    lax.fori_loop(0, 4, lay_two, 0)
-    for q in range(2):
-        a, b = place(0, q)
-        gb_ref[:, q * 128:q * 128 + 128] = two_all[a, b, 64:].astype(F32)[:1]
-    arrived(sums)
-
-    def mid_step(b, carry):
-        w_mid[b] = add_up(
-            w_out[u, b].astype(F32), [w_in[d, b] for d in range(SIDE - 1)]
-        ).astype(BF)
-        return carry
-
-    lax.fori_loop(0, SIDE, mid_step, 0)
-    sums = [send(w_mid.at[(v + e) % SIDE], v_in.at[e - 1], v_dev(e)) for e in others]
     arrived(sums)
     z_out[...] = add_up(w_mid[v].astype(F32), [v_in[e] for e in range(SIDE - 1)]).astype(BF)
     sums = [
         send(z_out.at[pl.ds(dz * 32, 32)], z_in.at[dz - 1], feat_dev(-dz, 0)) for dz in others
     ]
-    arrived([y_two_copy(e) for e in others])
-
-    def out_step(t, carry):
-        total = add_up(ysum_two[tile(t, 64)], [yrecv_two[e, tile(t, 64)] for e in range(3)])
-        out_ref[tile(t, 64)] = (self_two[tile(t, 64)] + b_two[...] + total / FAN).astype(BF)
-        return carry
-
-    lax.fori_loop(0, rows_three // 64, out_step, 0)
-
     arrived(sums)
     piece_all[u, v] = add_up(
         z_out[:32].astype(F32), [z_in[dz] for dz in range(3)]
@@ -489,6 +483,15 @@
     sums = [send(piece_all.at[u, v], piece_all.at[u, v], v_dev(e)) for e in others]
     arrived(sums)
     sums = [send(piece_all.at[u], piece_all.at[u], u_dev(d)) for d in others]
+    arrived([y_two_copy(e) for e in others])
+
+    def out_step(t, carry):
+        total = add_up(ysum_two[tile(t, 64)], [yrecv_two[e, tile(t, 64)] for e in range(3)])
+        out_ref[tile(t, 64)] = (self_two[tile(t, 64)] + b_two[...] + total / FAN).astype(BF)
+        return carry
+
+    lax.fori_loop(0, rows_three // 64, out_step, 0)
+
     arrived(sums)
 
     def lay_one(r, carry):
@@ -521,7 +524,6 @@
         two_v_copy(e).wait_send()
         y_two_copy(e).wait_send()
         back_two(e).wait_send()
-        back_copy(e).wait_send()
 
 
 def store_kernel(*refs):

time: 110 us -> 106 us (0.964)
  Pallas kernels: 110 us -> 105 us
    pallas_call x1, Pallas kernels: 107 us -> 103 us  [on_device(): pl.pallas_call(step_kernel, out_shape=[jax.ShapeDtypeStruct((r3, 256), BF...]
where the time goes in v9:
time: 106 us; the launch traced here: 105 us
  Pallas kernels  105 us (99%)
    pallas_call x1, Pallas kernels, on_device(): pl.pallas_call(step_kernel, out_shape=[jax.ShapeDtypeStruct((r3, 256), BF...  103 us

profile of v9, /device:TPU:0, one launch (start us, length us, event | category | flops | bytes accessed | tf_op | source)
XLA Modules:
  0.0 105.4 jit_solution(2990981222758503801)
XLA Ops:
  0.6 102.7 %sage_step.1 = (bf16[256,256]{1,0:T(8,128)(2,1)}, f32[128,512]{1,0:T(8,128)}, f32[256,512]{1,0:T(8,128)}, f32[1,256]{1,0:T(1,128)}) custom-call(bf16[8,1024,128]{2,1,0:T(8,128)(2,1)} %feat_ref.1, bf16[128,512]{1,0:T(8,128)(2,1)} %w_one_ref.1, bf16[256,512]{1,0:T(8,128)(2,1)} %w_two_ref.1, f32[1,256]{1,0:T(1,128)} %bitcast.23, f32[1,256]{1,0:T(1,128)} %bitcast.24, ...), custom_call_target="tpu_custom_call" | custom-call | flops 14000000000 | bytes 8388608 | tf_op jit(solution)/shard_map/sage_step/pallas_call | solution.py:569
  103.4 2.1 %store_results.1 = (bf16[256,256]{1,0:T(8,128)(2,1)}, f32[128,512]{1,0:T(8,128)}, f32[256,512]{1,0:T(8,128)}, f32[1,256]{1,0:T(1,128)}) custom-call(bf16[256,256]{1,0:T(8,128)(2,1)} %get-tuple-element.12.refs_0_, f32[128,512]{1,0:T(8,128)} %get-tuple-element.13.refs_1_, f32[256,512]{1,0:T(8,128)} %get-tuple-element.14.refs_2_, ...), custom_call_target="tpu_custom_call" | custom-call | tf_op jit(solution)/shard_map/store_results/pallas_call | solution.py:591

commit v10 on v9

--- a/solution.py
+++ b/solution.py
@@ -328,33 +328,33 @@
     for q in range(2):
         a, b = place(0, q)
         two_out[a, b, 64:] = jnp.broadcast_to(bias[:, q * 128:q * 128 + 128], (16, 128)).astype(BF)
+
+    proj = dot(hidden[...], w_two[...])
+    table_two[0] = proj[:, 256:].astype(BF)
+    self_two[...] = proj[:rows_three, :256]
+
+    two_v_at = group(3)
+    back_at = group(3)
+
+    def two_v_copy(e):
+        return describe(two_v_at + e - 1, two_mid.at[(v + e) % SIDE], two_v.at[e - 1], v_dev(e))
+
+    def back_copy(d):
+        return describe(back_at + d - 1, gsend.at[d - 1], grecv.at[d - 1], u_dev(-d))
+
+    def line_grads(e, d):
+        ids = lax.broadcasted_iota(I32, (rows_one, rows_two), 0)
+        return dot((ids == asks[e, pl.ds(d, 1), :rows_two]).astype(BF), msg_one[e])
+
+    def own_step(d, carry):
+        gsum[d] = line_grads(0, d)
+        return carry
+
+    lax.fori_loop(0, SIDE, own_step, 0)
+    arrived([msg_copy(h, e) for h in range(tiles) for e in others])
     two_u_copies = [
         send(two_out.at[(u + d) % SIDE], two_in.at[d - 1], u_dev(d)) for d in others
     ]
-
-    proj = dot(hidden[...], w_two[...])
-    table_two[0] = proj[:, 256:].astype(BF)
-    self_two[...] = proj[:rows_three, :256]
-
-    two_v_at = group(3)
-    back_at = group(3)
-
-    def two_v_copy(e):
-        return describe(two_v_at + e - 1, two_mid.at[(v + e) % SIDE], two_v.at[e - 1], v_dev(e))
-
-    def back_copy(d):
-        return describe(back_at + d - 1, gsend.at[d - 1], grecv.at[d - 1], u_dev(-d))
-
-    def line_grads(e, d):
-        ids = lax.broadcasted_iota(I32, (rows_one, rows_two), 0)
-        return dot((ids == asks[e, pl.ds(d, 1), :rows_two]).astype(BF), msg_one[e])
-
-    def own_step(d, carry):
-        gsum[d] = line_grads(0, d)
-        return carry
-
-    lax.fori_loop(0, SIDE, own_step, 0)
-    arrived([msg_copy(h, e) for h in range(tiles) for e in others])
 
     def back_step(j, carry):
         d = (j + 1) % SIDE

time: 106 us -> 104 us (0.981)
  Pallas kernels: 105 us -> 103 us
    pallas_call x1, Pallas kernels: 103 us -> 101 us  [on_device(): pl.pallas_call(step_kernel, out_shape=[jax.ShapeDtypeStruct((r3, 256), BF...]
where the time goes in v10:
time: 104 us
  Pallas kernels  103 us (99%)
    pallas_call x1, Pallas kernels, on_device(): pl.pallas_call(step_kernel, out_shape=[jax.ShapeDtypeStruct((r3, 256), BF...  101 us

profile of v10, /device:TPU:0, one launch (start us, length us, event | category | flops | bytes accessed | tf_op | source)
XLA Modules:
  0.0 103.6 jit_solution(9400865252710392361)
XLA Ops:
  0.6 100.9 %sage_step.1 = (bf16[256,256]{1,0:T(8,128)(2,1)}, f32[128,512]{1,0:T(8,128)}, f32[256,512]{1,0:T(8,128)}, f32[1,256]{1,0:T(1,128)}) custom-call(bf16[8,1024,128]{2,1,0:T(8,128)(2,1)} %feat_ref.1, bf16[128,512]{1,0:T(8,128)(2,1)} %w_one_ref.1, bf16[256,512]{1,0:T(8,128)(2,1)} %w_two_ref.1, f32[1,256]{1,0:T(1,128)} %bitcast.23, f32[1,256]{1,0:T(1,128)} %bitcast.24, ...), custom_call_target="tpu_custom_call" | custom-call | flops 14000000000 | bytes 8388608 | tf_op jit(solution)/shard_map/sage_step/pallas_call | solution.py:569
  101.5 2.1 %store_results.1 = (bf16[256,256]{1,0:T(8,128)(2,1)}, f32[128,512]{1,0:T(8,128)}, f32[256,512]{1,0:T(8,128)}, f32[1,256]{1,0:T(1,128)}) custom-call(bf16[256,256]{1,0:T(8,128)(2,1)} %get-tuple-element.12.refs_0_, f32[128,512]{1,0:T(8,128)} %get-tuple-element.13.refs_1_, f32[256,512]{1,0:T(8,128)} %get-tuple-element.14.refs_2_, ...), custom_call_target="tpu_custom_call" | custom-call | tf_op jit(solution)/shard_map/store_results/pallas_call | solution.py:591
